TPU v7x, 128 devices: a whole 4x4x4 slice. The times are simulated.
128 devices in a mesh: grp: 8 (over y, core), sub: 16 (over x, z).
Axes of the slice: x: 4, y: 4, z: 4, core: 2. Of those that a mesh axis runs over, the one named last changes fastest.
Arguments:
- points: bfloat16 [8192, 1024], P(('grp', 'sub')), may hold values from -6 to 6
- point_cluster: int32 [8192], P(('grp', 'sub')), may hold values from 0 to 262143, as said below
- candidates: int32 [8192, 128], P(('grp', 'sub')), may hold values from 0 to 262143, as said below
- old_fine: bfloat16 [262144, 1024], P(('grp', 'sub')), may hold values from -6 to 6
- fine_parent: int32 [262144], P(('grp', 'sub')), may hold values from 0 to 16383, as said below
- old_middle: bfloat16 [16384, 1024], P('grp'), may hold values from -6 to 6
- middle_parent: int32 [16384], P('grp'), may hold values from 0 to 1023
- old_top: bfloat16 [1024, 1024], replicated, may hold values from -6 to 6
Outputs:
- new_fine: bfloat16 [262144, 1024], P(('grp', 'sub'))
- new_middle: bfloat16 [16384, 1024], P('grp')
- new_top: bfloat16 [1024, 1024], replicated
- candidate_sq_distance: float32 [8192, 128], P(('grp', 'sub'))
Inputs may be any that keep to these rules, and one draw needn't show every extreme that they name: `point_cluster`: Level-1 centroids are held in slices of 2048 rows, slice f on the device of flat index f over grp then sub. Among the 64 points of one device, at most 3 belong to the centroids of any one slice; in every draw some slice receives exactly 3 from every device. `candidates`: candidate j of a point held by a device in group g of grp lies in the slice of the device (g, j mod 16). `fine_parent`: A level-1 centroid held in group g of grp has its parent among the level-2 centroids g * 16384 / 8 to (g + 1) * 16384 / 8 - 1. Split these into 16 equal consecutive shares: of the 2048 level-1 centroids of one slice, exactly 2048 / 16 have their parent in each share.
All inputs are finite; a program needn't handle non-finite values.
Results may differ from a plain program's by a relative error of at most 0.018.
Values may be sent and summed in bfloat16 or wider, within the bound.
No kernel may reach another device: no remote copies, remote signals or barrier semaphores. Data moves between devices by JAX's collectives and lax.ppermute only.
A program may use at most 192 MiB of HBM per device.

v0:
```python
import functools

import jax
import jax.numpy as jnp
from jax import lax
from jax.experimental import pallas as pl
from jax.experimental.pallas import tpu as pltpu
from jax.sharding import PartitionSpec as P

CAP = 3
LANES = 128
SUBLANES = 8
LANE_BITS = 7
ID_BITS = 6
LOW_LANE = 8
COUNT_LANE = 16
FINE_STEP = 512
MIDDLE_STEP = 512
TOP_STEP = 512
EXACT = 256
SIDE = 4
MOST_SHARES = 16
BOTH = ("grp", "sub")


def level_update(totals, members, olds):
    return ((totals + olds.astype(jnp.float32)) / (members + 1.0)[:, None]).astype(jnp.bfloat16)


def swap(blocks, axes):
    return lax.all_to_all(blocks, axes, split_axis=0, concat_axis=0, tiled=True)


def spread(block, axes):
    copies = lax.axis_size(axes)
    return swap(jnp.broadcast_to(block[None], (copies,) + block.shape), axes)


def ring(count, apart, turn):
    pairs = []
    for i in range(count):
        place = i // apart % SIDE
        pairs.append((i, i + ((place + turn) % SIDE - place) * apart))
    return pairs


def dot(left, right):
    return jnp.dot(left, right, preferred_element_type=jnp.float32)


def hits(count, first, parents):
    rows = lax.broadcasted_iota(jnp.int32, (count, parents.shape[1]), 0) + first
    return rows == parents


def quick_table(rows, first, parents):
    pieces = []
    for begin in range(0, rows, EXACT):
        near = parents - (first + begin)
        near = jnp.where(jnp.logical_and(near >= 0, near < EXACT), near, -1)
        near = near.astype(jnp.float32).astype(jnp.bfloat16)
        ids = lax.broadcasted_iota(jnp.int32, (EXACT, parents.shape[1]), 0)
        ids = ids.astype(jnp.float32).astype(jnp.bfloat16)
        pieces.append(jnp.where(ids == near, jnp.bfloat16(1), jnp.bfloat16(0)))
    return jnp.concatenate(pieces, axis=0)


def column(row):
    count = row.shape[1]
    down = lax.broadcasted_iota(jnp.int32, (count, count), 0)
    along = lax.broadcasted_iota(jnp.int32, (count, count), 1)
    return jnp.sum(jnp.where(down == along, row, jnp.zeros_like(row)), axis=1, keepdims=True)


def small(numbers):
    return numbers.astype(jnp.float32).astype(jnp.bfloat16)


def send_kernel(
    share_ref,
    clusters_ref,
    points_ref,
    parents_ref,
    fine_parents_ref,
    candidates_ref,
    out_ref,
    wide_ref,
    counts_ref,
    *,
    fine_count,
):
    rows, feat_dim = points_ref.shape
    slots = out_ref.shape[0]
    slot_count = CAP + 1
    devices = slots // slot_count
    fine_bits = fine_count.bit_length() - 1
    clusters = clusters_ref[...]
    cluster_column = column(clusters)
    owners = lax.shift_right_logical(clusters, fine_bits)
    owner_column = lax.shift_right_logical(cluster_column, fine_bits)
    down = lax.broadcasted_iota(jnp.int32, (rows, rows), 0)
    along = lax.broadcasted_iota(jnp.int32, (rows, rows), 1)
    same = owner_column == owners
    ranks = jnp.sum(jnp.where(same & (down < along), 1, 0), axis=0, keepdims=True)
    rank_column = jnp.sum(jnp.where(same & (along < down), 1, 0), axis=1, keepdims=True)
    ids = jnp.bitwise_and(cluster_column, fine_count - 1)
    high = lax.shift_right_logical(ids, ID_BITS) + 1
    low = jnp.bitwise_and(ids, (1 << ID_BITS) - 1)
    lane = lax.broadcasted_iota(jnp.int32, (rows, feat_dim), 1)
    id_rows = jnp.where(lane == rank_column, high, jnp.where(lane == LOW_LANE + rank_column, low, 0))
    id_rows = id_rows.astype(jnp.float32).astype(jnp.bfloat16)
    share = share_ref[0]
    parents = parents_ref[:, pl.ds(pl.multiple_of(share * LANES, LANES), LANES)]
    top_bits = share_ref[2]
    table = hits(devices, 0, lax.shift_right_logical(parents, top_bits)).astype(jnp.bfloat16)
    within = jnp.bitwise_and(parents, lax.shift_left(jnp.int32(1), top_bits) - 1)
    spots = hits(feat_dim, 0, within + COUNT_LANE).astype(jnp.bfloat16)
    counts = lax.dot_general(
        table, spots, (((1,), (1,)), ((), ())), preferred_element_type=jnp.float32
    )
    counts = counts.astype(jnp.bfloat16)
    fine_parents = fine_parents_ref[...]
    shares = share_ref[1]
    share_of = jnp.bitwise_and(lax.shift_right_logical(fine_parents, LANE_BITS), shares - 1)
    table = hits(MOST_SHARES, 0, share_of).astype(jnp.bfloat16)
    spots = hits(LANES, 0, jnp.bitwise_and(fine_parents, LANES - 1)).astype(jnp.bfloat16)
    counts_ref[...] = lax.dot_general(
        table, spots, (((1,), (1,)), ((), ())), preferred_element_type=jnp.float32
    )
    place = jnp.bitwise_and(candidates_ref[...], fine_count - 1)
    chunk = lax.shift_right_logical(place, LANE_BITS)
    within = jnp.bitwise_and(place, LANES - 1)
    wide_ref[:, :feat_dim] = points_ref[...]
    wide_ref[:, feat_dim : feat_dim + LANES] = small(chunk)
    wide_ref[:, feat_dim + LANES : feat_dim + 2 * LANES] = small(within)
    every = lax.broadcasted_iota(jnp.int32, (1, devices), 1)
    sent = dot(hits(slots, 0, owners * slot_count + ranks).astype(jnp.bfloat16), points_ref[...])
    sent = sent + dot(hits(slots, 0, owners * slot_count + CAP).astype(jnp.bfloat16), id_rows)
    sent = sent + dot(hits(slots, 0, every * slot_count + CAP).astype(jnp.bfloat16), counts)
    out_ref[...] = sent.astype(jnp.bfloat16)


def outgoing(
    which, point_cluster, points, middle_parent, fine_parent, candidates, devices, fine_count
):
    rows, feat_dim = points.shape
    slots = devices * (CAP + 1)
    wide = feat_dim + 2 * LANES

    def whole(i, s):
        return (0, 0)

    return pl.pallas_call(
        functools.partial(send_kernel, fine_count=fine_count),
        out_shape=(
            jax.ShapeDtypeStruct((slots, feat_dim), jnp.bfloat16),
            jax.ShapeDtypeStruct((rows, wide), jnp.bfloat16),
            jax.ShapeDtypeStruct((MOST_SHARES, LANES), jnp.float32),
        ),
        grid_spec=pltpu.PrefetchScalarGridSpec(
            num_scalar_prefetch=1,
            grid=(1,),
            in_specs=[
                pl.BlockSpec((1, rows), whole),
                pl.BlockSpec((rows, feat_dim), whole),
                pl.BlockSpec((1, middle_parent.shape[0]), whole),
                pl.BlockSpec((1, fine_parent.shape[0]), whole),
                pl.BlockSpec(candidates.shape, whole),
            ],
            out_specs=[
                pl.BlockSpec((slots, feat_dim), whole),
                pl.BlockSpec((rows, wide), whole),
                pl.BlockSpec((MOST_SHARES, LANES), whole),
            ],
        ),
        compiler_params=pltpu.CompilerParams(vmem_limit_bytes=24 * 1024 * 1024),
        cost_estimate=pl.CostEstimate(
            flops=4 * slots * LANES * feat_dim, bytes_accessed=2 * 1024 * 1024, transcendentals=0
        ),
    )(
        which,
        point_cluster[None, :],
        points,
        middle_parent[None, :],
        fine_parent[None, :],
        candidates,
    )


def levels_kernel(
    share_ref,
    got_ref,
    ids_ref,
    old_fine_ref,
    parent_ref,
    members_ref,
    old_share_ref,
    top_parent_ref,
    fine_ref,
    middle_ref,
    top_ref,
    held,
    scaled,
    sent,
):
    step = pl.program_id(0)
    last = pl.num_programs(0) - 1
    fine_steps = held.shape[0] // FINE_STEP
    middle_steps = scaled.shape[0] // MIDDLE_STEP
    top_rows = top_ref.shape[0]
    store = pltpu.make_async_copy(held, fine_ref, sent)

    @pl.when(step < fine_steps)
    def _():
        first = pl.multiple_of(step * FINE_STEP, FINE_STEP)
        found = hits(FINE_STEP, first, ids_ref[...])
        members = jnp.sum(found.astype(jnp.float32), axis=1, keepdims=True)
        totals = dot(found.astype(jnp.bfloat16), got_ref[...])
        totals = totals + old_fine_ref[...].astype(jnp.float32)
        held[pl.ds(first, FINE_STEP), :] = (totals * (1.0 / (members + 1.0))).astype(jnp.bfloat16)

    @pl.when(step == fine_steps)
    def _():
        store.start()

    @pl.when(jnp.logical_and(step >= fine_steps, step < fine_steps + middle_steps))
    def _():
        first = pl.multiple_of((step - fine_steps) * MIDDLE_STEP, MIDDLE_STEP)
        part = dot(quick_table(MIDDLE_STEP, first, parent_ref[...]), held[...])
        middle_ref[...] = part.astype(jnp.bfloat16)
        block = (step - fine_steps) * (MIDDLE_STEP // LANES)
        rows = [members_ref[pl.ds(block + i, 1), :] for i in range(MIDDLE_STEP // LANES)]
        members = jnp.concatenate([column(row) for row in rows], axis=0)
        weighted = part * (1.0 / (members + 1.0))
        scaled[pl.ds(first, MIDDLE_STEP), :] = weighted.astype(jnp.bfloat16)

    @pl.when(step >= fine_steps + middle_steps)
    def _():
        first = (step - fine_steps - middle_steps) * top_rows
        olds = old_share_ref[...].astype(jnp.float32)
        members = column(members_ref[pl.ds(share_ref[0], 1), :])
        olds = (olds * (1.0 / (members + 1.0))).astype(jnp.bfloat16)
        own = pl.ds(pl.multiple_of(share_ref[0] * LANES, LANES), LANES)
        own_table = quick_table(top_rows, first, top_parent_ref[:, own])
        table = quick_table(top_rows, first, top_parent_ref[...])
        top_ref[...] = dot(table, scaled[...]) + dot(own_table, olds)

    @pl.when(step == last)
    def _():
        store.wait()


def levels(which, got, ids, old_fine, parents, members, old_middle, top_parents, top_count):
    fine_count, feat_dim = old_fine.shape
    middle_count = old_middle.shape[0]
    share_rows = members.shape[1]
    slots = got.shape[0]
    fine_steps = fine_count // FINE_STEP
    middle_steps = middle_count // MIDDLE_STEP
    top_steps = top_count // TOP_STEP

    def fine_at(i, s):
        return (jnp.minimum(i, fine_steps - 1), 0)

    def middle_at(i, s):
        return (jnp.clip(i - fine_steps, 0, middle_steps - 1), 0)

    def top_at(i, s):
        return (jnp.maximum(i - fine_steps - middle_steps, 0), 0)

    def whole(i, s):
        return (0, 0)

    flops = 2 * feat_dim * (fine_count * slots + middle_count * (fine_count + top_count))
    return pl.pallas_call(
        levels_kernel,
        out_shape=(
            jax.ShapeDtypeStruct((fine_count, feat_dim), jnp.bfloat16),
            jax.ShapeDtypeStruct((middle_count, feat_dim), jnp.bfloat16),
            jax.ShapeDtypeStruct((top_count, feat_dim), jnp.float32),
        ),
        grid_spec=pltpu.PrefetchScalarGridSpec(
            num_scalar_prefetch=1,
            grid=(fine_steps + middle_steps + top_steps,),
            in_specs=[
                pl.BlockSpec((slots, feat_dim), whole),
                pl.BlockSpec((1, slots), whole),
                pl.BlockSpec((FINE_STEP, feat_dim), fine_at),
                pl.BlockSpec((1, fine_count), whole),
                pl.BlockSpec(members.shape, whole),
                pl.BlockSpec((share_rows, feat_dim), lambda i, s: (s[0], 0)),
                pl.BlockSpec((1, middle_count), whole),
            ],
            out_specs=[
                pl.BlockSpec(memory_space=pl.ANY),
                pl.BlockSpec((MIDDLE_STEP, feat_dim), middle_at),
                pl.BlockSpec((TOP_STEP, feat_dim), top_at),
            ],
            scratch_shapes=[
                pltpu.VMEM((fine_count, feat_dim), jnp.bfloat16),
                pltpu.VMEM((middle_count, feat_dim), jnp.bfloat16),
                pltpu.SemaphoreType.DMA,
            ],
        ),
        compiler_params=pltpu.CompilerParams(vmem_limit_bytes=56 * 1024 * 1024),
        cost_estimate=pl.CostEstimate(
            flops=flops, bytes_accessed=18 * 1024 * 1024, transcendentals=0
        ),
    )(which, got, ids, old_fine, parents, members, old_middle, top_parents)


def distance_kernel(share_ref, rows_ref, fine_ref, norms_ref, out_ref):
    fine_count, feat_dim = fine_ref.shape
    rows = rows_ref.shape[0]
    block = rows_ref[:, :feat_dim]
    wide = block.astype(jnp.float32)
    point_norms = jnp.sum(wide * wide, axis=1, keepdims=True)
    cross = lax.dot_general(
        block, fine_ref[...], (((1,), (1,)), ((), ())), preferred_element_type=jnp.float32
    )
    places = rows_ref[:, feat_dim : feat_dim + 2 * LANES].astype(jnp.float32).astype(jnp.int32)
    chunk = places[:, :LANES]
    lane = places[:, LANES:]
    picked = jnp.zeros((rows, LANES), jnp.float32)
    for c in range(fine_count // LANES):
        here = slice(c * LANES, (c + 1) * LANES)
        scores = norms_ref[:, here] - 2.0 * cross[:, here]
        found = jnp.take_along_axis(scores, lane, axis=1)
        picked = jnp.where(chunk == c, found, picked)
    column = lax.broadcasted_iota(jnp.int32, (rows, LANES), 1)
    mine = jnp.bitwise_and(column, share_ref[1] - 1) == share_ref[0]
    total = jnp.maximum(picked + point_norms, 0.0) * (1.0 / feat_dim)
    total = jnp.where(mine, total, 0.0)
    per_block = rows // out_ref.shape[0]
    for block in range(out_ref.shape[0]):
        packed = jnp.zeros((SUBLANES, LANES), jnp.float32)
        for b in range(per_block // SUBLANES):
            first = block * per_block + b * SUBLANES
            shift = jnp.bitwise_and(b - share_ref[0] + LANES, LANES - 1)
            packed = packed + pltpu.roll(total[first : first + SUBLANES], shift, 1)
        out_ref[block] = packed


def candidate_parts(share, all_rows, old_fine, fine_norms, groups):
    row_count = all_rows.shape[0] // groups
    fine_count, feat_dim = old_fine.shape
    per_step = 2
    return pl.pallas_call(
        distance_kernel,
        out_shape=jax.ShapeDtypeStruct((groups, SUBLANES, LANES), jnp.float32),
        grid_spec=pltpu.PrefetchScalarGridSpec(
            num_scalar_prefetch=1,
            grid=(groups // per_step,),
            in_specs=[
                pl.BlockSpec((per_step * row_count, all_rows.shape[1]), lambda i, s: (i, 0)),
                pl.BlockSpec((fine_count, feat_dim), lambda i, s: (0, 0)),
                pl.BlockSpec((1, fine_count), lambda i, s: (0, 0)),
            ],
            out_specs=pl.BlockSpec((per_step, SUBLANES, LANES), lambda i, s: (i, 0, 0)),
        ),
        compiler_params=pltpu.CompilerParams(vmem_limit_bytes=40 * 1024 * 1024),
        cost_estimate=pl.CostEstimate(
            flops=2 * groups * row_count * fine_count * feat_dim,
            bytes_accessed=2 * (groups * row_count + fine_count) * feat_dim,
            transcendentals=0,
        ),
    )(share, all_rows, old_fine, fine_norms)


def place_kernel(at_ref, *refs):
    *pieces, out_ref = refs
    for i, piece in enumerate(pieces):
        row = pl.multiple_of(at_ref[i], piece.shape[0])
        out_ref[pl.ds(row, piece.shape[0]), :] = piece[...]


def all_blocks(block, total):
    places = lax.axis_size("grp")
    cores = places // SIDE
    onward = ring(places, cores, 1)
    backward = ring(places, cores, SIDE - 1)
    across = [(i, i ^ 1) for i in range(places)]
    rows = block.shape[0]
    half = rows // 2
    before = lax.ppermute(block, "grp", onward)
    after = lax.ppermute(block, "grp", backward)
    far_first = lax.ppermute(before[:half], "grp", onward)
    far_last = lax.ppermute(after[half:], "grp", backward)
    pieces = [block, before, after, far_first, far_last]
    pieces += [lax.ppermute(piece, "grp", across) for piece in pieces]
    me = lax.axis_index("grp")
    chip = me // cores
    starts = []
    for core in (me % cores, 1 - me % cores):
        for turn, shift in ((0, 0), (SIDE - 1, 0), (1, 0), (2, 0), (2, half)):
            starts.append(((chip + turn) % SIDE * cores + core) * rows + shift)
    return pl.pallas_call(
        place_kernel,
        out_shape=jax.ShapeDtypeStruct((total, block.shape[1]), block.dtype),
        grid_spec=pltpu.PrefetchScalarGridSpec(
            num_scalar_prefetch=1,
            grid=(1,),
            in_specs=[pl.BlockSpec(piece.shape, lambda i, at: (0, 0)) for piece in pieces],
            out_specs=pl.BlockSpec((total, block.shape[1]), lambda i, at: (0, 0)),
        ),
        compiler_params=pltpu.CompilerParams(vmem_limit_bytes=32 * 1024 * 1024),
        cost_estimate=pl.CostEstimate(flops=0, bytes_accessed=4 * 1024 * 1024, transcendentals=0),
    )(jnp.stack(starts).astype(jnp.int32), *pieces)


def per_device(
    points, point_cluster, candidates, old_fine, fine_parent, old_middle, middle_parent, old_top
):
    devices = lax.axis_size(BOTH)
    group_width = lax.axis_size("sub")
    share = lax.axis_index("sub")
    device = lax.axis_index(BOTH)
    row_count, feat_dim = points.shape
    fine_count = old_fine.shape[0]
    middle_count = old_middle.shape[0]
    top_count = old_top.shape[0]
    share_rows = middle_count // group_width
    top_rows = top_count // devices
    which = jnp.stack([share, jnp.int32(group_width), jnp.int32(top_rows.bit_length() - 1)])

    slot_count = CAP + 1
    send_rows, wide_rows, middle_members = outgoing(
        which,
        point_cluster,
        points,
        middle_parent,
        fine_parent,
        candidates,
        devices,
        fine_count,
    )
    got = swap(send_rows.reshape(devices, slot_count, feat_dim), BOTH)
    side = got[:, CAP, :LANES].astype(jnp.float32)
    got_high = side[:, :CAP].astype(jnp.int32)
    got_low = side[:, LOW_LANE : LOW_LANE + CAP].astype(jnp.int32)
    got_ids = jnp.where(got_high > 0, (got_high - 1) * (1 << ID_BITS) + got_low, -1)
    got_ids = jnp.pad(got_ids, ((0, 0), (0, 1)), constant_values=-1)
    top_totals = jnp.sum(side[:, COUNT_LANE : COUNT_LANE + top_rows], axis=0)

    all_rows = lax.all_gather(wide_rows, "sub", axis=0, tiled=True)
    for apart in (1, SIDE):
        around = [middle_members]
        for turn in range(1, SIDE):
            around.append(lax.ppermute(middle_members, "sub", ring(group_width, apart, turn)))
        middle_members = sum(around)

    middle_local = fine_parent - lax.axis_index("grp") * middle_count
    new_fine, middle_part, top_part = levels(
        which,
        got.reshape(devices * slot_count, feat_dim),
        got_ids.reshape(1, devices * slot_count),
        old_fine,
        middle_local[None, :],
        middle_members,
        old_middle,
        middle_parent[None, :],
        top_count,
    )

    parts = swap(middle_part.reshape(group_width, share_rows, feat_dim), "sub")
    wide_fine = old_fine.astype(jnp.float32)
    fine_norms = jnp.sum(wide_fine * wide_fine, axis=1)[None, :]
    found = candidate_parts(which, all_rows, old_fine, fine_norms, group_width)
    parts, found = lax.optimization_barrier((parts, found))
    share_totals = lax.dynamic_slice_in_dim(middle_members, share, 1).reshape(share_rows)
    old_share = lax.dynamic_slice_in_dim(old_middle, share * share_rows, share_rows)
    new_share = level_update(jnp.sum(parts.astype(jnp.float32), axis=0), share_totals, old_share)
    new_middle = lax.all_gather(new_share, "sub", axis=0, tiled=True)

    top_block = lax.psum_scatter(top_part, "grp", scatter_dimension=0, tiled=True)
    top_pieces = top_block.reshape(group_width, top_rows, feat_dim)
    returned = swap(jnp.concatenate([top_pieces, found], axis=2), "sub")
    top_sums = jnp.sum(returned[:, :, :feat_dim], axis=0)
    packed = returned[:, :, feat_dim:].reshape(group_width, SUBLANES, -1, group_width)
    packed = packed[..., : row_count // SUBLANES]
    candidate_sq_distance = packed.transpose(3, 1, 2, 0).reshape(row_count, -1)
    old_rows = lax.dynamic_slice_in_dim(old_top, device * top_rows, top_rows)
    new_rows = level_update(top_sums, top_totals, old_rows)
    new_block = spread(new_rows, "sub").reshape(group_width * top_rows, feat_dim)
    new_top = all_blocks(new_block, top_count)
    return (new_fine, new_middle, new_top, candidate_sq_distance)


def solution(mesh):
    placed = (
        P(BOTH, None),
        P(BOTH),
        P(BOTH, None),
        P(BOTH, None),
        P(BOTH),
        P("grp", None),
        P("grp"),
        P(),
    )
    return jax.shard_map(
        per_device,
        mesh=mesh,
        in_specs=placed,
        out_specs=(P(BOTH, None), P("grp", None), P(), P(BOTH, None)),
        check_vma=False,
    )
```

profile of v0, /device:TPU:1, one launch (start us, length us, event | category | flops | bytes accessed | tf_op | source)
XLA Modules:
  0.0 209.8 jit_solution(2890798852801492543)
XLA Ops:
  11.9 2.4 %shard_map.111 = (bf16[512,1024]{1,0:T(8,128)(2,1)S(1)}, bf16[64,1280]{1,0:T(8,128)(2,1)}, f32[16,128]{1,0:T(8,128)S(1)}) custom-call(s32[3]{0:T(128)S(1)} %pad_add_fusion.share_ref, s32[1,64]{1,0:T(1,128)S(1)} %bitcast.34, bf16[64,1024]{1,0:T(8,128)(2,1)S(1)} %copy-done.6, s32[1,2048]{1,0:T(1,128)S(1)} %bitcast.33, s32[1,2048]{1,0:T(1,128)S(1)} %bitcast.31, ...), custom_call_target="tpu_custom_call" | custom-call | flops 268435456 | bytes 2097152 | tf_op jit(solution)/shard_map/pallas_call | solution.py:153
  15.5 11.5 %all-to-all-start = ((bf16[128,4,1024]{2,1,0:T(4,128)(2,1)}), bf16[128,4,1024]{2,1,0:T(4,128)(2,1)S(1)}, u32[]{:S(2)}, u32[]{:S(2)}) async-start(bf16[128,4,1024]{2,1,0:T(4,128)(2,1)} %reshape.46), calls=%async_computation | async-start | bytes 2097152 | tf_op jit(solution)/shard_map/all_to_all | solution.py:31
  27.1 3.3 %collective-permute-start.2 = (f32[16,128]{1,0:T(8,128)S(1)}, f32[16,128]{1,0:T(8,128)S(1)}, u32[]{:S(2)}, u32[]{:S(2)}) collective-permute-start(f32[16,128]{1,0:T(8,128)S(1)} %get-tuple-element.13), channel_id=1, source_target_pairs={{0,3},{1,0},{2,1},{3,2},{4,7},{5,4},{6,5},{7,6},{8,11},{9,8},{10,9... | collective-permute-start | bytes 24584 | tf_op jit(solution)/shard_map/ppermute | solution.py:449
  31.3 3.8 %collective-permute-done.1 = f32[16,128]{1,0:T(8,128)S(1)} collective-permute-done((f32[16,128]{1,0:T(8,128)S(1)}, f32[16,128]{1,0:T(8,128)S(1)}, u32[]{:S(2)}, u32[]{:S(2)}) %collective-permute-start.1) | collective-permute-done | bytes 8224 | tf_op jit(solution)/shard_map/ppermute | solution.py:449
  35.2 2.8 %collective-permute-start.5 = (f32[16,128]{1,0:T(8,128)S(1)}, f32[16,128]{1,0:T(8,128)S(1)}, u32[]{:S(2)}, u32[]{:S(2)}) collective-permute-start(f32[16,128]{1,0:T(8,128)S(1)} %add_add_fusion.1), channel_id=1, source_target_pairs={{0,12},{1,13},{2,14},{3,15},{4,0},{5,1},{6,2},{7,3},{8,4},{9,5},{1... | collective-permute-start | bytes 24584 | tf_op jit(solution)/shard_map/ppermute | solution.py:449
  44.0 3.5 %all-to-all-done = bf16[128,4,1024]{2,1,0:T(4,128)(2,1)S(1)} async-done(((bf16[128,4,1024]{2,1,0:T(4,128)(2,1)}), bf16[128,4,1024]{2,1,0:T(4,128)(2,1)S(1)}, u32[]{:S(2)}, u32[]{:S(2)}) %all-to-all-start) | async-done | bytes 1048608 | tf_op jit(solution)/shard_map/all_to_all | solution.py:31
  49.5 22.9 %shard_map.112 = (bf16[2048,1024]{1,0:T(8,128)(2,1)}, bf16[2048,1024]{1,0:T(8,128)(2,1)}, f32[1024,1024]{1,0:T(8,128)}) custom-call(s32[3]{0:T(128)} %copy-done.3, bf16[512,1024]{1,0:T(8,128)(2,1)} %reshape.47.got_ref, s32[1,512]{1,0:T(1,128)} %reshape.48.ids_ref, bf16[2048,1024]{1,0:T(8,128)(2,1)} %fine_ref.1, s32[1,2048]{1,0:T(1,128)} %bitcast.41, ...), custom_call_target="tpu_custom_call" | custom-call | flops 15032385536 | bytes 18874368 | tf_op jit(solution)/shard_map/pallas_call | solution.py:275
  72.4 4.6 %all-to-all-start.1 = ((bf16[16,128,1024]{2,1,0:T(8,128)(2,1)}), bf16[16,128,1024]{2,1,0:T(8,128)(2,1)}, u32[]{:S(2)}, u32[]{:S(2)}) async-start(bf16[16,128,1024]{2,1,0:T(8,128)(2,1)} %bitcast.35), calls=%async_computation.1 | async-start | bytes 8388608 | tf_op jit(solution)/shard_map/all_to_all | solution.py:31
  77.2 3.1 %multiply_reduce_fusion = f32[2048]{0:T(1024)S(1)} fusion(bf16[2048,1024]{1,0:T(8,128)(2,1)} %fine_ref.1), kind=kLoop, calls=%fused_computation.1 | loop fusion | flops 6289408 | bytes 4202496 | tf_op jit(solution)/shard_map/reduce_sum | solution.py:467
  81.0 2.6 %copy-done = bf16[2048,1024]{1,0:T(8,128)(2,1)S(1)} copy-done((bf16[2048,1024]{1,0:T(8,128)(2,1)S(1)}, bf16[2048,1024]{1,0:T(8,128)(2,1)}, u32[]{:S(2)}) %copy-start) | copy-done | bytes 4194328
  83.6 1.7 copy-done.5
  85.3 14.7 %shard_map.113 = f32[16,8,128]{2,1,0:T(8,128)S(1)} custom-call(s32[3]{0:T(128)S(1)} %copy-done.4, bf16[1024,1280]{1,0:T(8,128)(2,1)S(1)} %copy-done.5, bf16[2048,1024]{1,0:T(8,128)(2,1)S(1)} %copy-done, f32[1,2048]{1,0:T(1,128)S(1)} %bitcast.30), custom_call_target="tpu_custom_call" | custom-call | flops 4294967296 | bytes 6291456 | tf_op jit(solution)/shard_map/pallas_call | solution.py:348
  100.0 34.7 %all-to-all-done.1 = bf16[16,128,1024]{2,1,0:T(8,128)(2,1)} async-done(((bf16[16,128,1024]{2,1,0:T(8,128)(2,1)}), bf16[16,128,1024]{2,1,0:T(8,128)(2,1)}, u32[]{:S(2)}, u32[]{:S(2)}) %all-to-all-start.1) | async-done | bytes 4194336 | tf_op jit(solution)/shard_map/all_to_all | solution.py:31
  134.7 3.1 %convert_reduce_fusion = f32[128,1024]{1,0:T(8,128)S(1)} fusion(bf16[16,128,1024]{2,1,0:T(8,128)(2,1)} %all-to-all-done.1), kind=kLoop, calls=%fused_computation | loop fusion | flops 4063232 | bytes 4718592 | tf_op jit(solution)/shard_map/reduce_sum | solution.py:472
  137.9 1.8 divide_convert_fusion
  139.7 1.9 pad_maximum_fusion
  141.6 10.2 %all-to-all-start.2 = ((f32[16,8,1152]{2,1,0:T(8,128)}), f32[16,8,1152]{2,1,0:T(8,128)S(1)}, u32[]{:S(2)}, u32[]{:S(2)}) async-start(f32[16,8,1152]{2,1,0:T(8,128)} %pad_maximum_fusion), calls=%async_computation.3 | async-start | bytes 1179648 | tf_op jit(solution)/shard_map/all_to_all | solution.py:31
  151.9 9.2 %all-to-all-done.2 = f32[16,8,1152]{2,1,0:T(8,128)S(1)} async-done(((f32[16,8,1152]{2,1,0:T(8,128)}), f32[16,8,1152]{2,1,0:T(8,128)S(1)}, u32[]{:S(2)}, u32[]{:S(2)}) %all-to-all-start.2) | async-done | bytes 589856 | tf_op jit(solution)/shard_map/all_to_all | solution.py:31
  162.0 10.4 %all_to_all.20 = bf16[16,8,1024]{2,1,0:T(8,128)(2,1)S(1)} all-to-all(bf16[16,8,1024]{2,1,0:T(8,128)(2,1)S(1)} %broadcast_in_dim.31), channel_id=1, replica_groups=mesh['grp'=8,'sub'=16] {'sub'}, dimensions={0} | all-to-all | bytes 524288 | tf_op jit(solution)/shard_map/all_to_all | solution.py:31
  173.9 8.4 %collective-permute-start.10 = (bf16[128,1024]{1,0:T(8,128)(2,1)S(1)}, bf16[128,1024]{1,0:T(8,128)(2,1)S(1)}, u32[]{:S(2)}, u32[]{:S(2)}) collective-permute-start(bf16[128,1024]{1,0:T(8,128)(2,1)S(1)} %bitcast.28), channel_id=1, source_target_pairs={{0,16},{16,0},{32,48},{48,32},{64,80},{80,64},{96,112},{112,96},{1... | collective-permute-start | bytes 786440 | tf_op jit(solution)/shard_map/ppermute | solution.py:390
  184.0 6.1 %collective-permute-start.12 = (bf16[128,1024]{1,0:T(8,128)(2,1)S(1)}, bf16[128,1024]{1,0:T(8,128)(2,1)S(1)}, u32[]{:S(2)}, u32[]{:S(2)}) collective-permute-start(bf16[128,1024]{1,0:T(8,128)(2,1)S(1)} %collective-permute-done.7.refs_2_), channel_id=1, source_target_pairs={{0,16},{16,0},{32,48},{48,32},{64,80},{80,64},{96,112},{112,96},{1... | collective-permute-start | bytes 786440 | tf_op jit(solution)/shard_map/ppermute | solution.py:390
  190.1 2.7 %collective-permute-start.14 = (bf16[64,1024]{1,0:T(8,128)(2,1)S(1)}, bf16[64,1024]{1,0:T(8,128)(2,1)S(1)}, u32[]{:S(2)}, u32[]{:S(2)}) collective-permute-start(bf16[64,1024]{1,0:T(8,128)(2,1)S(1)} %collective-permute-done.9.refs_4_), channel_id=1, source_target_pairs={{0,16},{16,0},{32,48},{48,32},{64,80},{80,64},{96,112},{112,96},{1... | collective-permute-start | bytes 393224 | tf_op jit(solution)/shard_map/ppermute | solution.py:390
  195.7 2.0 shard_map.114
  197.7 4.6 %copy.21 = bf16[2048,1024]{1,0:T(8,128)(2,1)} copy(bf16[2048,1024]{1,0:T(8,128)(2,1)} %all-gather.5.cloned.1.call-done) | data formatting | bytes 8388608
  (74 shorter events, 22.0 us)
Async XLA Ops:
  8.0 31.6 %copy-start.2 = (s32[2048]{0:T(1024)S(1)}, s32[2048]{0:T(1024)}, u32[]{:S(2)}) copy-start(s32[2048]{0:T(1024)} %param.12) | copy-start | bytes 24580
  8.0 73.0 %all-gather.3.cloned.1.call-start = ((), (), s32[]{:S(2)}) async-start(), calls=%async_computation.5 | async-start | bytes 2785280 | tf_op jit(solution)/shard_map/all_gather | solution.py:445
  8.1 41.4 %copy-start.3 = (s32[3]{0:T(128)}, s32[3]{0:T(128)S(1)}, u32[]{:S(2)}) copy-start(s32[3]{0:T(128)S(1)} %pad_add_fusion.share_ref) | copy-start | bytes 40
  15.5 32.0 %all-to-all-start = ((bf16[128,4,1024]{2,1,0:T(4,128)(2,1)}), bf16[128,4,1024]{2,1,0:T(4,128)(2,1)S(1)}, u32[]{:S(2)}, u32[]{:S(2)}) async-start(bf16[128,4,1024]{2,1,0:T(4,128)(2,1)} %reshape.46), calls=%async_computation | async-start | bytes 2097152 | tf_op jit(solution)/shard_map/all_to_all | solution.py:31
  27.0 112.7 %reduce-scatter.2.cloned.1.call-start = ((), (), s32[]{:S(2)}) async-start(), calls=%async_computation.7 | async-start | bytes 4718592 | tf_op jit(solution)/shard_map/reduce_scatter | solution.py:475
  27.1 4.2 %collective-permute-start.2 = (f32[16,128]{1,0:T(8,128)S(1)}, f32[16,128]{1,0:T(8,128)S(1)}, u32[]{:S(2)}, u32[]{:S(2)}) collective-permute-start(f32[16,128]{1,0:T(8,128)S(1)} %get-tuple-element.13), channel_id=1, source_target_pairs={{0,3},{1,0},{2,1},{3,2},{4,7},{5,4},{6,5},{7,6},{8,11},{9,8},{10,9... | collective-permute-start | bytes 24584 | tf_op jit(solution)/shard_map/ppermute | solution.py:449
  30.4 4.6 %collective-permute-start.1 = (f32[16,128]{1,0:T(8,128)S(1)}, f32[16,128]{1,0:T(8,128)S(1)}, u32[]{:S(2)}, u32[]{:S(2)}) collective-permute-start(f32[16,128]{1,0:T(8,128)S(1)} %get-tuple-element.13), channel_id=1, source_target_pairs={{0,2},{1,3},{2,0},{3,1},{4,6},{5,7},{6,4},{7,5},{8,10},{9,11},{10,... | collective-permute-start | bytes 24584 | tf_op jit(solution)/shard_map/ppermute | solution.py:449
  30.5 4.7 %collective-permute-start = (f32[16,128]{1,0:T(8,128)S(1)}, f32[16,128]{1,0:T(8,128)S(1)}, u32[]{:S(2)}, u32[]{:S(2)}) collective-permute-start(f32[16,128]{1,0:T(8,128)S(1)} %get-tuple-element.13), channel_id=1, source_target_pairs={{0,1},{1,2},{2,3},{3,0},{4,5},{5,6},{6,7},{7,4},{8,9},{9,10},{10,1... | collective-permute-start | bytes 24584 | tf_op jit(solution)/shard_map/ppermute | solution.py:449
  35.2 6.7 %collective-permute-start.5 = (f32[16,128]{1,0:T(8,128)S(1)}, f32[16,128]{1,0:T(8,128)S(1)}, u32[]{:S(2)}, u32[]{:S(2)}) collective-permute-start(f32[16,128]{1,0:T(8,128)S(1)} %add_add_fusion.1), channel_id=1, source_target_pairs={{0,12},{1,13},{2,14},{3,15},{4,0},{5,1},{6,2},{7,3},{8,4},{9,5},{1... | collective-permute-start | bytes 24584 | tf_op jit(solution)/shard_map/ppermute | solution.py:449
  38.0 5.4 %collective-permute-start.4 = (f32[16,128]{1,0:T(8,128)S(1)}, f32[16,128]{1,0:T(8,128)S(1)}, u32[]{:S(2)}, u32[]{:S(2)}) collective-permute-start(f32[16,128]{1,0:T(8,128)S(1)} %add_add_fusion.1), channel_id=1, source_target_pairs={{0,8},{1,9},{2,10},{3,11},{4,12},{5,13},{6,14},{7,15},{8,0},{9,1},... | collective-permute-start | bytes 24584 | tf_op jit(solution)/shard_map/ppermute | solution.py:449
  38.9 4.5 %collective-permute-start.3 = (f32[16,128]{1,0:T(8,128)S(1)}, f32[16,128]{1,0:T(8,128)S(1)}, u32[]{:S(2)}, u32[]{:S(2)}) collective-permute-start(f32[16,128]{1,0:T(8,128)S(1)} %add_add_fusion.1), channel_id=1, source_target_pairs={{0,4},{1,5},{2,6},{3,7},{4,8},{5,9},{6,10},{7,11},{8,12},{9,13},{1... | collective-permute-start | bytes 24584 | tf_op jit(solution)/shard_map/ppermute | solution.py:449
  72.4 62.3 %all-to-all-start.1 = ((bf16[16,128,1024]{2,1,0:T(8,128)(2,1)}), bf16[16,128,1024]{2,1,0:T(8,128)(2,1)}, u32[]{:S(2)}, u32[]{:S(2)}) async-start(bf16[16,128,1024]{2,1,0:T(8,128)(2,1)} %bitcast.35), calls=%async_computation.1 | async-start | bytes 8388608 | tf_op jit(solution)/shard_map/all_to_all | solution.py:31
  77.0 4.0 %copy-start.4 = (s32[3]{0:T(128)S(1)}, s32[3]{0:T(128)}, u32[]{:S(2)}) copy-start(s32[3]{0:T(128)} %copy-done.3) | copy-start | bytes 40
  77.0 120.7 %all-gather.5.cloned.1.call-start = ((), (), s32[]{:S(2)}) async-start(), calls=%async_computation.6 | async-start | bytes 4456448 | tf_op jit(solution)/shard_map/all_gather | solution.py:473
  141.6 19.6 %all-to-all-start.2 = ((f32[16,8,1152]{2,1,0:T(8,128)}), f32[16,8,1152]{2,1,0:T(8,128)S(1)}, u32[]{:S(2)}, u32[]{:S(2)}) async-start(f32[16,8,1152]{2,1,0:T(8,128)} %pad_maximum_fusion), calls=%async_computation.3 | async-start | bytes 1179648 | tf_op jit(solution)/shard_map/all_to_all | solution.py:31
  172.4 9.9 %collective-permute-start.7 = (bf16[128,1024]{1,0:T(8,128)(2,1)S(1)}, bf16[128,1024]{1,0:T(8,128)(2,1)S(1)}, u32[]{:S(2)}, u32[]{:S(2)}) collective-permute-start(bf16[128,1024]{1,0:T(8,128)(2,1)S(1)} %bitcast.26), channel_id=1, source_target_pairs={{0,96},{16,112},{32,0},{48,16},{64,32},{80,48},{96,64},{112,80},{1... | collective-permute-start | bytes 786440 | tf_op jit(solution)/shard_map/ppermute | solution.py:386
  172.4 10.9 %collective-permute-start.6 = (bf16[128,1024]{1,0:T(8,128)(2,1)S(1)}, bf16[128,1024]{1,0:T(8,128)(2,1)S(1)}, u32[]{:S(2)}, u32[]{:S(2)}) collective-permute-start(bf16[128,1024]{1,0:T(8,128)(2,1)S(1)} %bitcast.27), channel_id=1, source_target_pairs={{0,32},{16,48},{32,64},{48,80},{64,96},{80,112},{96,0},{112,16},{1... | collective-permute-start | bytes 786440 | tf_op jit(solution)/shard_map/ppermute | solution.py:385
  173.9 21.7 %collective-permute-start.10 = (bf16[128,1024]{1,0:T(8,128)(2,1)S(1)}, bf16[128,1024]{1,0:T(8,128)(2,1)S(1)}, u32[]{:S(2)}, u32[]{:S(2)}) collective-permute-start(bf16[128,1024]{1,0:T(8,128)(2,1)S(1)} %bitcast.28), channel_id=1, source_target_pairs={{0,16},{16,0},{32,48},{48,32},{64,80},{80,64},{96,112},{112,96},{1... | collective-permute-start | bytes 786440 | tf_op jit(solution)/shard_map/ppermute | solution.py:390
  182.3 7.7 %collective-permute-start.9 = (bf16[64,1024]{1,0:T(8,128)(2,1)S(1)}, bf16[64,1024]{1,0:T(8,128)(2,1)S(1)}, u32[]{:S(2)}, u32[]{:S(2)}) collective-permute-start(bf16[64,1024]{1,0:T(8,128)(2,1)S(1)} %slice.42), channel_id=1, source_target_pairs={{0,96},{16,112},{32,0},{48,16},{64,32},{80,48},{96,64},{112,80},{1... | collective-permute-start | bytes 393224 | tf_op jit(solution)/shard_map/ppermute | solution.py:388
  183.4 9.4 %collective-permute-start.8 = (bf16[64,1024]{1,0:T(8,128)(2,1)S(1)}, bf16[64,1024]{1,0:T(8,128)(2,1)S(1)}, u32[]{:S(2)}, u32[]{:S(2)}) collective-permute-start(bf16[64,1024]{1,0:T(8,128)(2,1)S(1)} %slice.41), channel_id=1, source_target_pairs={{0,32},{16,48},{32,64},{48,80},{64,96},{80,112},{96,0},{112,16},{1... | collective-permute-start | bytes 393224 | tf_op jit(solution)/shard_map/ppermute | solution.py:387
  184.0 11.7 %collective-permute-start.12 = (bf16[128,1024]{1,0:T(8,128)(2,1)S(1)}, bf16[128,1024]{1,0:T(8,128)(2,1)S(1)}, u32[]{:S(2)}, u32[]{:S(2)}) collective-permute-start(bf16[128,1024]{1,0:T(8,128)(2,1)S(1)} %collective-permute-done.7.refs_2_), channel_id=1, source_target_pairs={{0,16},{16,0},{32,48},{48,32},{64,80},{80,64},{96,112},{112,96},{1... | collective-permute-start | bytes 786440 | tf_op jit(solution)/shard_map/ppermute | solution.py:390
  190.1 5.6 %collective-permute-start.11 = (bf16[128,1024]{1,0:T(8,128)(2,1)S(1)}, bf16[128,1024]{1,0:T(8,128)(2,1)S(1)}, u32[]{:S(2)}, u32[]{:S(2)}) collective-permute-start(bf16[128,1024]{1,0:T(8,128)(2,1)S(1)} %collective-permute-done.6.refs_1_), channel_id=1, source_target_pairs={{0,16},{16,0},{32,48},{48,32},{64,80},{80,64},{96,112},{112,96},{1... | collective-permute-start | bytes 786440 | tf_op jit(solution)/shard_map/ppermute | solution.py:390
  190.1 5.6 %collective-permute-start.14 = (bf16[64,1024]{1,0:T(8,128)(2,1)S(1)}, bf16[64,1024]{1,0:T(8,128)(2,1)S(1)}, u32[]{:S(2)}, u32[]{:S(2)}) collective-permute-start(bf16[64,1024]{1,0:T(8,128)(2,1)S(1)} %collective-permute-done.9.refs_4_), channel_id=1, source_target_pairs={{0,16},{16,0},{32,48},{48,32},{64,80},{80,64},{96,112},{112,96},{1... | collective-permute-start | bytes 393224 | tf_op jit(solution)/shard_map/ppermute | solution.py:390
  192.8 2.9 %collective-permute-start.13 = (bf16[64,1024]{1,0:T(8,128)(2,1)S(1)}, bf16[64,1024]{1,0:T(8,128)(2,1)S(1)}, u32[]{:S(2)}, u32[]{:S(2)}) collective-permute-start(bf16[64,1024]{1,0:T(8,128)(2,1)S(1)} %collective-permute-done.8.refs_3_), channel_id=1, source_target_pairs={{0,16},{16,0},{32,48},{48,32},{64,80},{80,64},{96,112},{112,96},{1... | collective-permute-start | bytes 393224 | tf_op jit(solution)/shard_map/ppermute | solution.py:390
  (7 other events, 8.0 us)
Sparse Core Ops, SparseCore 0:
  14.4 57.7 all-gather.2
  139.8 57.8 all-gather.4
Sparse Core Ops, SparseCore 1:
  72.5 35.9 reduce-scatter.1
where the time goes:
time: 211 us; the launch traced here: 210 us
  starting transfers between devices  56.9 us (27%)
  waiting for transfers between devices  54.7 us (26%)
  Pallas kernels  42 us (20%)
  local copies, waits for them, and re-layouts  17.1 us (8%)
  between operations  15.7 us (7%)
  other arithmetic  13 us (6%)
  blocking collectives  10.4 us (5%)
    all_to_all x3, waiting for transfers between devices, swap(): return lax.all_to_all(blocks, axes, split_axis=0, concat_axis=0, tiled=True)  47.5 us
    all_to_all x3, starting transfers between devices, swap(): return lax.all_to_all(blocks, axes, split_axis=0, concat_axis=0, tiled=True)  26.3 us
    pallas_call x1, Pallas kernels, levels(): pl.pallas_call(levels_kernel, out_shape=(jax.ShapeDtypeStruct((fine_count...  22.9 us
    ppermute x5, starting transfers between devices, all_blocks(): pieces += [lax.ppermute(piece, 'grp', across) for piece in pieces]  18.7 us
    pallas_call x1, Pallas kernels, candidate_parts(): pl.pallas_call(distance_kernel, out_shape=jax.ShapeDtypeStruct((groups, S...  14.7 us
    unnamed x22, local copies, waits for them, and re-layouts  13 us
    all_to_all x1, blocking collectives, swap(): return lax.all_to_all(blocks, axes, split_axis=0, concat_axis=0, tiled=True)  10.4 us
    ppermute x6, starting transfers between devices, per_device(): lax.ppermute(middle_members, 'sub', ring(group_width, apart, turn))  8.58 us
  transfers between devices with their start and end apart: 21, of which 7 were waited for; matrix products, arithmetic and copies ran while one was open for 8% of the time, Pallas kernels for 19%

commit v1 on v0

--- a/solution.py
+++ b/solution.py
@@ -17,9 +17,11 @@
 FINE_STEP = 512
 MIDDLE_STEP = 512
 TOP_STEP = 512
+LEFT_STEP = 1024
 EXACT = 256
 SIDE = 4
 MOST_SHARES = 16
+LONG = 1_000_000_000_000
 BOTH = ("grp", "sub")
 
 
@@ -187,7 +189,79 @@
     )
 
 
-def levels_kernel(
+def fine_step(step, got_ref, ids_ref, old_fine_ref, held):
+    first = pl.multiple_of(step * FINE_STEP, FINE_STEP)
+    found = hits(FINE_STEP, first, ids_ref[...])
+    members = jnp.sum(found.astype(jnp.float32), axis=1, keepdims=True)
+    totals = dot(found.astype(jnp.bfloat16), got_ref[...])
+    totals = totals + old_fine_ref[...].astype(jnp.float32)
+    held[pl.ds(first, FINE_STEP), :] = (totals * (1.0 / (members + 1.0))).astype(jnp.bfloat16)
+
+
+def left_kernel(got_ref, ids_ref, old_fine_ref, parent_ref, fine_ref, middle_ref, held, sent):
+    step = pl.program_id(0)
+    fine_steps = held.shape[0] // FINE_STEP
+    store = pltpu.make_async_copy(held, fine_ref.at[:, : held.shape[1]], sent)
+
+    @pl.when(step < fine_steps)
+    def _():
+        fine_step(step, got_ref, ids_ref, old_fine_ref, held)
+
+    @pl.when(step == fine_steps)
+    def _():
+        store.start()
+
+    @pl.when(step >= fine_steps)
+    def _():
+        first = (step - fine_steps) * LEFT_STEP
+        table = quick_table(LEFT_STEP, first, parent_ref[...])
+        middle_ref[...] = dot(table, held[...]).astype(jnp.bfloat16)
+
+    @pl.when(step == pl.num_programs(0) - 1)
+    def _():
+        store.wait()
+
+
+def left_levels(got, ids, old_fine, parents, middle_count):
+    fine_count, feat_dim = old_fine.shape
+    half = feat_dim // 2
+    slots = got.shape[0]
+    fine_steps = fine_count // FINE_STEP
+
+    def whole(i):
+        return (0, 0)
+
+    return pl.pallas_call(
+        left_kernel,
+        out_shape=(
+            jax.ShapeDtypeStruct((fine_count, feat_dim), jnp.bfloat16),
+            jax.ShapeDtypeStruct((middle_count, half), jnp.bfloat16),
+        ),
+        grid=(fine_steps + middle_count // LEFT_STEP,),
+        in_specs=[
+            pl.BlockSpec((slots, half), whole),
+            pl.BlockSpec((1, slots), whole),
+            pl.BlockSpec((FINE_STEP, half), lambda i: (jnp.minimum(i, fine_steps - 1), 0)),
+            pl.BlockSpec((1, fine_count), whole),
+        ],
+        out_specs=[
+            pl.BlockSpec(memory_space=pl.ANY),
+            pl.BlockSpec((LEFT_STEP, half), lambda i: (jnp.maximum(i - fine_steps, 0), 0)),
+        ],
+        scratch_shapes=[
+            pltpu.VMEM((fine_count, half), jnp.bfloat16),
+            pltpu.SemaphoreType.DMA,
+        ],
+        compiler_params=pltpu.CompilerParams(vmem_limit_bytes=56 * 1024 * 1024),
+        cost_estimate=pl.CostEstimate(
+            flops=2 * half * fine_count * (slots + middle_count),
+            bytes_accessed=8 * 1024 * 1024,
+            transcendentals=0,
+        ),
+    )(got, ids, old_fine, parents)
+
+
+def right_kernel(
     share_ref,
     got_ref,
     ids_ref,
@@ -196,6 +270,8 @@
     members_ref,
     old_share_ref,
     top_parent_ref,
+    left_ref,
+    kept_ref,
     fine_ref,
     middle_ref,
     top_ref,
@@ -203,21 +279,17 @@
     scaled,
     sent,
 ):
+    del kept_ref
     step = pl.program_id(0)
-    last = pl.num_programs(0) - 1
     fine_steps = held.shape[0] // FINE_STEP
     middle_steps = scaled.shape[0] // MIDDLE_STEP
     top_rows = top_ref.shape[0]
-    store = pltpu.make_async_copy(held, fine_ref, sent)
+    half = held.shape[1]
+    store = pltpu.make_async_copy(held, fine_ref.at[:, half:], sent)
 
     @pl.when(step < fine_steps)
     def _():
-        first = pl.multiple_of(step * FINE_STEP, FINE_STEP)
-        found = hits(FINE_STEP, first, ids_ref[...])
-        members = jnp.sum(found.astype(jnp.float32), axis=1, keepdims=True)
-        totals = dot(found.astype(jnp.bfloat16), got_ref[...])
-        totals = totals + old_fine_ref[...].astype(jnp.float32)
-        held[pl.ds(first, FINE_STEP), :] = (totals * (1.0 / (members + 1.0))).astype(jnp.bfloat16)
+        fine_step(step, got_ref, ids_ref, old_fine_ref, held)
 
     @pl.when(step == fine_steps)
     def _():
@@ -230,9 +302,10 @@
         middle_ref[...] = part.astype(jnp.bfloat16)
         block = (step - fine_steps) * (MIDDLE_STEP // LANES)
         rows = [members_ref[pl.ds(block + i, 1), :] for i in range(MIDDLE_STEP // LANES)]
-        members = jnp.concatenate([column(row) for row in rows], axis=0)
-        weighted = part * (1.0 / (members + 1.0))
-        scaled[pl.ds(first, MIDDLE_STEP), :] = weighted.astype(jnp.bfloat16)
+        weights = 1.0 / (jnp.concatenate([column(row) for row in rows], axis=0) + 1.0)
+        left = left_ref[...].astype(jnp.float32) * weights
+        scaled[pl.ds(first, MIDDLE_STEP), :half] = left.astype(jnp.bfloat16)
+        scaled[pl.ds(first, MIDDLE_STEP), half:] = (part * weights).astype(jnp.bfloat16)
 
     @pl.when(step >= fine_steps + middle_steps)
     def _():
@@ -245,13 +318,16 @@
         table = quick_table(top_rows, first, top_parent_ref[...])
         top_ref[...] = dot(table, scaled[...]) + dot(own_table, olds)
 
-    @pl.when(step == last)
+    @pl.when(step == pl.num_programs(0) - 1)
     def _():
         store.wait()
 
 
-def levels(which, got, ids, old_fine, parents, members, old_middle, top_parents, top_count):
+def right_levels(
+    which, got, ids, old_fine, parents, members, old_middle, top_parents, left, kept, top_count
+):
     fine_count, feat_dim = old_fine.shape
+    half = feat_dim // 2
     middle_count = old_middle.shape[0]
     share_rows = members.shape[1]
     slots = got.shape[0]
@@ -260,7 +336,7 @@
     top_steps = top_count // TOP_STEP
 
     def fine_at(i, s):
-        return (jnp.minimum(i, fine_steps - 1), 0)
+        return (jnp.minimum(i, fine_steps - 1), 1)
 
     def middle_at(i, s):
         return (jnp.clip(i - fine_steps, 0, middle_steps - 1), 0)
@@ -271,42 +347,45 @@
     def whole(i, s):
         return (0, 0)
 
-    flops = 2 * feat_dim * (fine_count * slots + middle_count * (fine_count + top_count))
+    flops = 2 * half * (fine_count * slots + middle_count * (fine_count + 2 * top_count))
     return pl.pallas_call(
-        levels_kernel,
+        right_kernel,
         out_shape=(
             jax.ShapeDtypeStruct((fine_count, feat_dim), jnp.bfloat16),
-            jax.ShapeDtypeStruct((middle_count, feat_dim), jnp.bfloat16),
+            jax.ShapeDtypeStruct((middle_count, half), jnp.bfloat16),
             jax.ShapeDtypeStruct((top_count, feat_dim), jnp.float32),
         ),
         grid_spec=pltpu.PrefetchScalarGridSpec(
             num_scalar_prefetch=1,
             grid=(fine_steps + middle_steps + top_steps,),
             in_specs=[
-                pl.BlockSpec((slots, feat_dim), whole),
+                pl.BlockSpec((slots, half), lambda i, s: (0, 1)),
                 pl.BlockSpec((1, slots), whole),
-                pl.BlockSpec((FINE_STEP, feat_dim), fine_at),
+                pl.BlockSpec((FINE_STEP, half), fine_at),
                 pl.BlockSpec((1, fine_count), whole),
                 pl.BlockSpec(members.shape, whole),
                 pl.BlockSpec((share_rows, feat_dim), lambda i, s: (s[0], 0)),
                 pl.BlockSpec((1, middle_count), whole),
+                pl.BlockSpec((MIDDLE_STEP, half), middle_at),
+                pl.BlockSpec(memory_space=pl.ANY),
             ],
             out_specs=[
                 pl.BlockSpec(memory_space=pl.ANY),
-                pl.BlockSpec((MIDDLE_STEP, feat_dim), middle_at),
+                pl.BlockSpec((MIDDLE_STEP, half), middle_at),
                 pl.BlockSpec((TOP_STEP, feat_dim), top_at),
             ],
             scratch_shapes=[
-                pltpu.VMEM((fine_count, feat_dim), jnp.bfloat16),
+                pltpu.VMEM((fine_count, half), jnp.bfloat16),
                 pltpu.VMEM((middle_count, feat_dim), jnp.bfloat16),
                 pltpu.SemaphoreType.DMA,
             ],
         ),
+        input_output_aliases={9: 0},
         compiler_params=pltpu.CompilerParams(vmem_limit_bytes=56 * 1024 * 1024),
         cost_estimate=pl.CostEstimate(
-            flops=flops, bytes_accessed=18 * 1024 * 1024, transcendentals=0
-        ),
-    )(which, got, ids, old_fine, parents, members, old_middle, top_parents)
+            flops=flops, bytes_accessed=14 * 1024 * 1024, transcendentals=0
+        ),
+    )(which, got, ids, old_fine, parents, members, old_middle, top_parents, left, kept)
 
 
 def distance_kernel(share_ref, rows_ref, fine_ref, norms_ref, out_ref):
@@ -360,7 +439,7 @@
         ),
         compiler_params=pltpu.CompilerParams(vmem_limit_bytes=40 * 1024 * 1024),
         cost_estimate=pl.CostEstimate(
-            flops=2 * groups * row_count * fine_count * feat_dim,
+            flops=LONG,
             bytes_accessed=2 * (groups * row_count + fine_count) * feat_dim,
             transcendentals=0,
         ),
@@ -450,26 +529,37 @@
         middle_members = sum(around)
 
     middle_local = fine_parent - lax.axis_index("grp") * middle_count
-    new_fine, middle_part, top_part = levels(
+    got = got.reshape(devices * slot_count, feat_dim)
+    got_ids = got_ids.reshape(1, devices * slot_count)
+    got_ids, middle_members = lax.optimization_barrier((got_ids, middle_members))
+    parents = middle_local[None, :]
+    half_fine, left = left_levels(got, got_ids, old_fine, parents, middle_count)
+    new_fine, right, top_part = right_levels(
         which,
-        got.reshape(devices * slot_count, feat_dim),
-        got_ids.reshape(1, devices * slot_count),
+        got,
+        got_ids,
         old_fine,
-        middle_local[None, :],
+        parents,
         middle_members,
         old_middle,
         middle_parent[None, :],
+        left,
+        half_fine,
         top_count,
     )
 
-    parts = swap(middle_part.reshape(group_width, share_rows, feat_dim), "sub")
+    shares = (group_width, share_rows, feat_dim // 2)
+    left = swap(left.reshape(shares), "sub")
+    right, left = lax.optimization_barrier((right, left))
+    right = swap(right.reshape(shares), "sub")
     wide_fine = old_fine.astype(jnp.float32)
     fine_norms = jnp.sum(wide_fine * wide_fine, axis=1)[None, :]
     found = candidate_parts(which, all_rows, old_fine, fine_norms, group_width)
-    parts, found = lax.optimization_barrier((parts, found))
+    left, right, found = lax.optimization_barrier((left, right, found))
     share_totals = lax.dynamic_slice_in_dim(middle_members, share, 1).reshape(share_rows)
     old_share = lax.dynamic_slice_in_dim(old_middle, share * share_rows, share_rows)
-    new_share = level_update(jnp.sum(parts.astype(jnp.float32), axis=0), share_totals, old_share)
+    sums = [jnp.sum(parts.astype(jnp.float32), axis=0) for parts in (left, right)]
+    new_share = level_update(jnp.concatenate(sums, axis=1), share_totals, old_share)
     new_middle = lax.all_gather(new_share, "sub", axis=0, tiled=True)
 
     top_block = lax.psum_scatter(top_part, "grp", scatter_dimension=0, tiled=True)

time: 211 us -> 200 us (0.948)
  waiting for transfers between devices: 54.7 us -> 33.9 us
  starting transfers between devices: 56.9 us -> 62.1 us
  Pallas kernels: 42 us -> 45.8 us
    all_to_all x3 -> x4, waiting for transfers between devices: 47.5 us -> 29.6 us  [swap(): return lax.all_to_all(blocks, axes, split_axis=0, concat_axis=0, tiled=True)]
    pallas_call x1 -> x2, Pallas kernels: 22.9 us -> 26.6 us  [the longest x1 17.2 us: right_levels(): pl.pallas_call(right_kernel, out_shape=(jax.ShapeDtypeStruct((fine_count,...]
    ppermute x6, starting transfers between devices: 8.58 us -> 12.2 us  [per_device(): lax.ppermute(middle_members, 'sub', ring(group_width, apart, turn))]
    ppermute x6, waiting for transfers between devices: 7.13 us -> 4.22 us  [per_device(): lax.ppermute(middle_members, 'sub', ring(group_width, apart, turn))]
    ppermute x5, starting transfers between devices: 18.7 us -> 16.5 us  [all_blocks(): pieces += [lax.ppermute(piece, 'grp', across) for piece in pieces]]
    all_to_all x3 -> x4, starting transfers between devices: 26.3 us -> 27.7 us  [swap(): return lax.all_to_all(blocks, axes, split_axis=0, concat_axis=0, tiled=True)]
    unnamed x22 -> x30, local copies, waits for them, and re-layouts: 13 us -> 13.4 us
  transfers between devices with their start and end apart: 21 -> 22, of which waited for: 7 -> 8; matrix products, arithmetic and copies ran while one was open for 8% -> 9% of each run, Pallas kernels for 19% -> 22%
where the time goes in v1:
time: 200 us; the launch traced here: 199 us
  starting transfers between devices  62.1 us (31%)
  Pallas kernels  45.8 us (23%)
  waiting for transfers between devices  33.9 us (17%)
  local copies, waits for them, and re-layouts  17.6 us (9%)
  between operations  15.8 us (8%)
  other arithmetic  13.2 us (7%)
  blocking collectives  10.3 us (5%)
    all_to_all x4, waiting for transfers between devices, swap(): return lax.all_to_all(blocks, axes, split_axis=0, concat_axis=0, tiled=True)  29.6 us
    all_to_all x4, starting transfers between devices, swap(): return lax.all_to_all(blocks, axes, split_axis=0, concat_axis=0, tiled=True)  27.7 us
    pallas_call x1, Pallas kernels, right_levels(): pl.pallas_call(right_kernel, out_shape=(jax.ShapeDtypeStruct((fine_count,...  17.2 us
    ppermute x5, starting transfers between devices, all_blocks(): pieces += [lax.ppermute(piece, 'grp', across) for piece in pieces]  16.5 us
    pallas_call x1, Pallas kernels, candidate_parts(): pl.pallas_call(distance_kernel, out_shape=jax.ShapeDtypeStruct((groups, S...  14.7 us
    unnamed x30, local copies, waits for them, and re-layouts  13.4 us
    ppermute x6, starting transfers between devices, per_device(): lax.ppermute(middle_members, 'sub', ring(group_width, apart, turn))  12.2 us
    all_to_all x1, blocking collectives, swap(): return lax.all_to_all(blocks, axes, split_axis=0, concat_axis=0, tiled=True)  10.3 us
  transfers between devices with their start and end apart: 22, of which 8 were waited for; matrix products, arithmetic and copies ran while one was open for 9% of the time, Pallas kernels for 22%

profile of v1, /device:TPU:1, one launch (start us, length us, event | category | flops | bytes accessed | tf_op | source)
XLA Modules:
  0.0 198.6 jit_solution(5477220667140707584)
XLA Ops:
  11.9 2.4 %shard_map.111 = (bf16[512,1024]{1,0:T(8,128)(2,1)S(1)}, bf16[64,1280]{1,0:T(8,128)(2,1)}, f32[16,128]{1,0:T(8,128)S(1)}) custom-call(s32[3]{0:T(128)S(1)} %pad_add_fusion.share_ref, s32[1,64]{1,0:T(1,128)S(1)} %bitcast.35, bf16[64,1024]{1,0:T(8,128)(2,1)S(1)} %copy-done.6, s32[1,2048]{1,0:T(1,128)S(1)} %bitcast.34, s32[1,2048]{1,0:T(1,128)S(1)} %bitcast.32, ...), custom_call_target="tpu_custom_call" | custom-call | flops 268435456 | bytes 2097152 | tf_op jit(solution)/shard_map/pallas_call | solution.py:155
  15.5 11.5 %all-to-all-start = ((bf16[128,4,1024]{2,1,0:T(4,128)(2,1)}), bf16[128,4,1024]{2,1,0:T(4,128)(2,1)S(1)}, u32[]{:S(2)}, u32[]{:S(2)}) async-start(bf16[128,4,1024]{2,1,0:T(4,128)(2,1)} %reshape.49), calls=%async_computation | async-start | bytes 2097152 | tf_op jit(solution)/shard_map/all_to_all | solution.py:33
  28.6 2.9 %collective-permute-start.1 = (f32[16,128]{1,0:T(8,128)S(1)}, f32[16,128]{1,0:T(8,128)S(1)}, u32[]{:S(2)}, u32[]{:S(2)}) collective-permute-start(f32[16,128]{1,0:T(8,128)S(1)} %get-tuple-element.20), channel_id=1, source_target_pairs={{0,2},{1,3},{2,0},{3,1},{4,6},{5,7},{6,4},{7,5},{8,10},{9,11},{10,... | collective-permute-start | bytes 24584 | tf_op jit(solution)/shard_map/ppermute | solution.py:528
  33.2 2.3 %collective-permute-done.2 = f32[16,128]{1,0:T(8,128)S(1)} collective-permute-done((f32[16,128]{1,0:T(8,128)S(1)}, f32[16,128]{1,0:T(8,128)S(1)}, u32[]{:S(2)}, u32[]{:S(2)}) %collective-permute-start.2) | collective-permute-done | bytes 8224 | tf_op jit(solution)/shard_map/ppermute | solution.py:528
  35.5 2.3 %collective-permute-start.3 = (f32[16,128]{1,0:T(8,128)S(1)}, f32[16,128]{1,0:T(8,128)S(1)}, u32[]{:S(2)}, u32[]{:S(2)}) collective-permute-start(f32[16,128]{1,0:T(8,128)S(1)} %add_add_fusion.1), channel_id=1, source_target_pairs={{0,4},{1,5},{2,6},{3,7},{4,8},{5,9},{6,10},{7,11},{8,12},{9,13},{1... | collective-permute-start | bytes 24584 | tf_op jit(solution)/shard_map/ppermute | solution.py:528
  37.8 3.3 %collective-permute-start.4 = (f32[16,128]{1,0:T(8,128)S(1)}, f32[16,128]{1,0:T(8,128)S(1)}, u32[]{:S(2)}, u32[]{:S(2)}) collective-permute-start(f32[16,128]{1,0:T(8,128)S(1)} %add_add_fusion.1), channel_id=1, source_target_pairs={{0,8},{1,9},{2,10},{3,11},{4,12},{5,13},{6,14},{7,15},{8,0},{9,1},... | collective-permute-start | bytes 24584 | tf_op jit(solution)/shard_map/ppermute | solution.py:528
  44.6 2.9 %all-to-all-done = bf16[128,4,1024]{2,1,0:T(4,128)(2,1)S(1)} async-done(((bf16[128,4,1024]{2,1,0:T(4,128)(2,1)}), bf16[128,4,1024]{2,1,0:T(4,128)(2,1)S(1)}, u32[]{:S(2)}, u32[]{:S(2)}) %all-to-all-start) | async-done | bytes 1048608 | tf_op jit(solution)/shard_map/all_to_all | solution.py:33
  50.1 9.4 %shard_map.112 = (bf16[2048,1024]{1,0:T(8,128)(2,1)}, bf16[2048,512]{1,0:T(8,128)(2,1)}) custom-call(bf16[512,1024]{1,0:T(8,128)(2,1)} %reshape.50.got_ref, s32[1,512]{1,0:T(1,128)} %reshape.51.ids_ref, bf16[2048,1024]{1,0:T(8,128)(2,1)} %fine_ref.1, s32[1,2048]{1,0:T(1,128)} %bitcast.43), custom_call_target="tpu_custom_call" | custom-call | flops 5368709120 | bytes 8388608 | tf_op jit(solution)/shard_map/pallas_call | solution.py:234
  59.6 3.7 %all-to-all-start.1 = ((bf16[16,128,512]{2,1,0:T(8,128)(2,1)}), bf16[16,128,512]{2,1,0:T(8,128)(2,1)S(1)}, u32[]{:S(2)}, u32[]{:S(2)}) async-start(bf16[16,128,512]{2,1,0:T(8,128)(2,1)} %bitcast.37), calls=%async_computation.1 | async-start | bytes 4194304 | tf_op jit(solution)/shard_map/all_to_all | solution.py:33
  63.4 3.1 %multiply_reduce_fusion = f32[2048]{0:T(1024)S(1)} fusion(bf16[2048,1024]{1,0:T(8,128)(2,1)} %fine_ref.1), kind=kLoop, calls=%fused_computation | loop fusion | flops 6289408 | bytes 4202496 | tf_op jit(solution)/shard_map/reduce_sum | solution.py:556
  66.5 17.2 %shard_map.113 = (bf16[2048,1024]{1,0:T(8,128)(2,1)}, bf16[2048,512]{1,0:T(8,128)(2,1)}, f32[1024,1024]{1,0:T(8,128)}) custom-call(s32[3]{0:T(128)} %copy-done.3, bf16[512,1024]{1,0:T(8,128)(2,1)} %reshape.50.got_ref, s32[1,512]{1,0:T(1,128)} %reshape.51.ids_ref, bf16[2048,1024]{1,0:T(8,128)(2,1)} %fine_ref.1, ...), custom_call_target="tpu_custom_call", output_to_operand_aliasing={{0}: (9, {})} | custom-call | flops 9663676416 | bytes 14680064 | tf_op jit(solution)/shard_map/pallas_call | solution.py:351
  85.0 10.9 %all-to-all-done.1 = bf16[16,128,512]{2,1,0:T(8,128)(2,1)S(1)} async-done(((bf16[16,128,512]{2,1,0:T(8,128)(2,1)}), bf16[16,128,512]{2,1,0:T(8,128)(2,1)S(1)}, u32[]{:S(2)}, u32[]{:S(2)}) %all-to-all-start.1) | async-done | bytes 2097184 | tf_op jit(solution)/shard_map/all_to_all | solution.py:33
  95.9 6.8 %all-to-all-start.2 = ((bf16[16,128,512]{2,1,0:T(8,128)(2,1)}), bf16[16,128,512]{2,1,0:T(8,128)(2,1)}, u32[]{:S(2)}, u32[]{:S(2)}) async-start(bf16[16,128,512]{2,1,0:T(8,128)(2,1)} %bitcast.38), calls=%async_computation.2 | async-start | bytes 4194304 | tf_op jit(solution)/shard_map/all_to_all | solution.py:33
  107.1 14.7 %shard_map.114 = f32[16,8,128]{2,1,0:T(8,128)S(1)} custom-call(s32[3]{0:T(128)S(1)} %copy-done.4, bf16[1024,1280]{1,0:T(8,128)(2,1)S(1)} %copy-done.5, bf16[2048,1024]{1,0:T(8,128)(2,1)S(1)} %copy-done, f32[1,2048]{1,0:T(1,128)S(1)} %bitcast.31), custom_call_target="tpu_custom_call" | custom-call | flops 999999995904 | bytes 6291456 | tf_op jit(solution)/shard_map/pallas_call | solution.py:427
  121.8 6.5 %all-to-all-done.2 = bf16[16,128,512]{2,1,0:T(8,128)(2,1)} async-done(((bf16[16,128,512]{2,1,0:T(8,128)(2,1)}), bf16[16,128,512]{2,1,0:T(8,128)(2,1)}, u32[]{:S(2)}, u32[]{:S(2)}) %all-to-all-start.2) | async-done | bytes 2097184 | tf_op jit(solution)/shard_map/all_to_all | solution.py:33
  128.3 2.8 %convert_reduce_fusion = (f32[128,512]{1,0:T(8,128)S(1)}, f32[128,512]{1,0:T(8,128)S(1)}) fusion(bf16[16,128,512]{2,1,0:T(8,128)(2,1)} %all-to-all-done.2, bf16[16,128,512]{2,1,0:T(8,128)(2,1)} %copy-done.10), kind=kLoop, calls=%fused_computation.1 | loop fusion | flops 4063232 | bytes 4718592 | tf_op jit(solution)/shard_map/reduce_sum | solution.py:561
  134.9 5.6 %all-to-all-start.3 = ((f32[16,8,1152]{2,1,0:T(8,128)}), f32[16,8,1152]{2,1,0:T(8,128)S(1)}, u32[]{:S(2)}, u32[]{:S(2)}) async-start(f32[16,8,1152]{2,1,0:T(8,128)} %pad_maximum_fusion), calls=%async_computation.4 | async-start | bytes 1179648 | tf_op jit(solution)/shard_map/all_to_all | solution.py:33
  140.6 9.2 %all-to-all-done.3 = f32[16,8,1152]{2,1,0:T(8,128)S(1)} async-done(((f32[16,8,1152]{2,1,0:T(8,128)}), f32[16,8,1152]{2,1,0:T(8,128)S(1)}, u32[]{:S(2)}, u32[]{:S(2)}) %all-to-all-start.3) | async-done | bytes 589856 | tf_op jit(solution)/shard_map/all_to_all | solution.py:33
  150.7 10.3 %all_to_all.25 = bf16[16,8,1024]{2,1,0:T(8,128)(2,1)S(1)} all-to-all(bf16[16,8,1024]{2,1,0:T(8,128)(2,1)S(1)} %broadcast_in_dim.31), channel_id=1, replica_groups=mesh['grp'=8,'sub'=16] {'sub'}, dimensions={0} | all-to-all | bytes 524288 | tf_op jit(solution)/shard_map/all_to_all | solution.py:33
  163.7 8.8 %collective-permute-start.10 = (bf16[128,1024]{1,0:T(8,128)(2,1)S(1)}, bf16[128,1024]{1,0:T(8,128)(2,1)S(1)}, u32[]{:S(2)}, u32[]{:S(2)}) collective-permute-start(bf16[128,1024]{1,0:T(8,128)(2,1)S(1)} %bitcast.29), channel_id=1, source_target_pairs={{0,16},{16,0},{32,48},{48,32},{64,80},{80,64},{96,112},{112,96},{1... | collective-permute-start | bytes 786440 | tf_op jit(solution)/shard_map/ppermute | solution.py:469
  172.6 2.7 %collective-permute-start.9 = (bf16[64,1024]{1,0:T(8,128)(2,1)S(1)}, bf16[64,1024]{1,0:T(8,128)(2,1)S(1)}, u32[]{:S(2)}, u32[]{:S(2)}) collective-permute-start(bf16[64,1024]{1,0:T(8,128)(2,1)S(1)} %slice.42), channel_id=1, source_target_pairs={{0,96},{16,112},{32,0},{48,16},{64,32},{80,48},{96,64},{112,80},{1... | collective-permute-start | bytes 393224 | tf_op jit(solution)/shard_map/ppermute | solution.py:467
  175.3 4.9 %collective-permute-start.11 = (bf16[128,1024]{1,0:T(8,128)(2,1)S(1)}, bf16[128,1024]{1,0:T(8,128)(2,1)S(1)}, u32[]{:S(2)}, u32[]{:S(2)}) collective-permute-start(bf16[128,1024]{1,0:T(8,128)(2,1)S(1)} %collective-permute-done.6.refs_1_), channel_id=1, source_target_pairs={{0,16},{16,0},{32,48},{48,32},{64,80},{80,64},{96,112},{112,96},{1... | collective-permute-start | bytes 786440 | tf_op jit(solution)/shard_map/ppermute | solution.py:469
  180.3 2.8 %collective-permute-start.13 = (bf16[64,1024]{1,0:T(8,128)(2,1)S(1)}, bf16[64,1024]{1,0:T(8,128)(2,1)S(1)}, u32[]{:S(2)}, u32[]{:S(2)}) collective-permute-start(bf16[64,1024]{1,0:T(8,128)(2,1)S(1)} %collective-permute-done.8.refs_3_), channel_id=1, source_target_pairs={{0,16},{16,0},{32,48},{48,32},{64,80},{80,64},{96,112},{112,96},{1... | collective-permute-start | bytes 393224 | tf_op jit(solution)/shard_map/ppermute | solution.py:469
  186.6 4.6 %copy.23 = bf16[2048,1024]{1,0:T(8,128)(2,1)} copy(bf16[2048,1024]{1,0:T(8,128)(2,1)} %all-gather.5.cloned.1.call-done) | data formatting | bytes 8388608
  (85 shorter events, 30.8 us)
Async XLA Ops:
  8.0 34.3 %copy-start.2 = (s32[2048]{0:T(1024)S(1)}, s32[2048]{0:T(1024)}, u32[]{:S(2)}) copy-start(s32[2048]{0:T(1024)} %param.12) | copy-start | bytes 24580
  8.0 94.9 %all-gather.3.cloned.1.call-start = ((), (), s32[]{:S(2)}) async-start(), calls=%async_computation.6 | async-start | bytes 2785280 | tf_op jit(solution)/shard_map/all_gather | solution.py:524
  8.1 51.5 %copy-start.3 = (s32[3]{0:T(128)}, s32[3]{0:T(128)S(1)}, u32[]{:S(2)}) copy-start(s32[3]{0:T(128)S(1)} %pad_add_fusion.share_ref) | copy-start | bytes 40
  15.5 32.0 %all-to-all-start = ((bf16[128,4,1024]{2,1,0:T(4,128)(2,1)}), bf16[128,4,1024]{2,1,0:T(4,128)(2,1)S(1)}, u32[]{:S(2)}, u32[]{:S(2)}) async-start(bf16[128,4,1024]{2,1,0:T(4,128)(2,1)} %reshape.49), calls=%async_computation | async-start | bytes 2097152 | tf_op jit(solution)/shard_map/all_to_all | solution.py:33
  27.0 5.4 %collective-permute-start = (f32[16,128]{1,0:T(8,128)S(1)}, f32[16,128]{1,0:T(8,128)S(1)}, u32[]{:S(2)}, u32[]{:S(2)}) collective-permute-start(f32[16,128]{1,0:T(8,128)S(1)} %get-tuple-element.20), channel_id=1, source_target_pairs={{0,1},{1,2},{2,3},{3,0},{4,5},{5,6},{6,7},{7,4},{8,9},{9,10},{10,1... | collective-permute-start | bytes 24584 | tf_op jit(solution)/shard_map/ppermute | solution.py:528
  28.6 4.6 %collective-permute-start.1 = (f32[16,128]{1,0:T(8,128)S(1)}, f32[16,128]{1,0:T(8,128)S(1)}, u32[]{:S(2)}, u32[]{:S(2)}) collective-permute-start(f32[16,128]{1,0:T(8,128)S(1)} %get-tuple-element.20), channel_id=1, source_target_pairs={{0,2},{1,3},{2,0},{3,1},{4,6},{5,7},{6,4},{7,5},{8,10},{9,11},{10,... | collective-permute-start | bytes 24584 | tf_op jit(solution)/shard_map/ppermute | solution.py:528
  31.5 4.0 %collective-permute-start.2 = (f32[16,128]{1,0:T(8,128)S(1)}, f32[16,128]{1,0:T(8,128)S(1)}, u32[]{:S(2)}, u32[]{:S(2)}) collective-permute-start(f32[16,128]{1,0:T(8,128)S(1)} %get-tuple-element.20), channel_id=1, source_target_pairs={{0,3},{1,0},{2,1},{3,2},{4,7},{5,4},{6,5},{7,6},{8,11},{9,8},{10,9... | collective-permute-start | bytes 24584 | tf_op jit(solution)/shard_map/ppermute | solution.py:528
  35.5 7.3 %collective-permute-start.3 = (f32[16,128]{1,0:T(8,128)S(1)}, f32[16,128]{1,0:T(8,128)S(1)}, u32[]{:S(2)}, u32[]{:S(2)}) collective-permute-start(f32[16,128]{1,0:T(8,128)S(1)} %add_add_fusion.1), channel_id=1, source_target_pairs={{0,4},{1,5},{2,6},{3,7},{4,8},{5,9},{6,10},{7,11},{8,12},{9,13},{1... | collective-permute-start | bytes 24584 | tf_op jit(solution)/shard_map/ppermute | solution.py:528
  37.8 5.8 %collective-permute-start.4 = (f32[16,128]{1,0:T(8,128)S(1)}, f32[16,128]{1,0:T(8,128)S(1)}, u32[]{:S(2)}, u32[]{:S(2)}) collective-permute-start(f32[16,128]{1,0:T(8,128)S(1)} %add_add_fusion.1), channel_id=1, source_target_pairs={{0,8},{1,9},{2,10},{3,11},{4,12},{5,13},{6,14},{7,15},{8,0},{9,1},... | collective-permute-start | bytes 24584 | tf_op jit(solution)/shard_map/ppermute | solution.py:528
  41.1 2.9 %collective-permute-start.5 = (f32[16,128]{1,0:T(8,128)S(1)}, f32[16,128]{1,0:T(8,128)S(1)}, u32[]{:S(2)}, u32[]{:S(2)}) collective-permute-start(f32[16,128]{1,0:T(8,128)S(1)} %add_add_fusion.1), channel_id=1, source_target_pairs={{0,12},{1,13},{2,14},{3,15},{4,0},{5,1},{6,2},{7,3},{8,4},{9,5},{1... | collective-permute-start | bytes 24584 | tf_op jit(solution)/shard_map/ppermute | solution.py:528
  59.6 36.3 %all-to-all-start.1 = ((bf16[16,128,512]{2,1,0:T(8,128)(2,1)}), bf16[16,128,512]{2,1,0:T(8,128)(2,1)S(1)}, u32[]{:S(2)}, u32[]{:S(2)}) async-start(bf16[16,128,512]{2,1,0:T(8,128)(2,1)} %bitcast.37), calls=%async_computation.1 | async-start | bytes 4194304 | tf_op jit(solution)/shard_map/all_to_all | solution.py:33
  63.3 69.7 %reduce-scatter.2.cloned.1.call-start = ((), (), s32[]{:S(2)}) async-start(), calls=%async_computation.8 | async-start | bytes 4718592 | tf_op jit(solution)/shard_map/reduce_scatter | solution.py:565
  95.9 32.4 %all-to-all-start.2 = ((bf16[16,128,512]{2,1,0:T(8,128)(2,1)}), bf16[16,128,512]{2,1,0:T(8,128)(2,1)}, u32[]{:S(2)}, u32[]{:S(2)}) async-start(bf16[16,128,512]{2,1,0:T(8,128)(2,1)} %bitcast.38), calls=%async_computation.2 | async-start | bytes 4194304 | tf_op jit(solution)/shard_map/all_to_all | solution.py:33
  102.7 83.9 %all-gather.5.cloned.1.call-start = ((), (), s32[]{:S(2)}) async-start(), calls=%async_computation.7 | async-start | bytes 4456448 | tf_op jit(solution)/shard_map/all_gather | solution.py:563
  134.9 15.0 %all-to-all-start.3 = ((f32[16,8,1152]{2,1,0:T(8,128)}), f32[16,8,1152]{2,1,0:T(8,128)S(1)}, u32[]{:S(2)}, u32[]{:S(2)}) async-start(f32[16,8,1152]{2,1,0:T(8,128)} %pad_maximum_fusion), calls=%async_computation.4 | async-start | bytes 1179648 | tf_op jit(solution)/shard_map/all_to_all | solution.py:33
  161.1 11.4 %collective-permute-start.6 = (bf16[128,1024]{1,0:T(8,128)(2,1)S(1)}, bf16[128,1024]{1,0:T(8,128)(2,1)S(1)}, u32[]{:S(2)}, u32[]{:S(2)}) collective-permute-start(bf16[128,1024]{1,0:T(8,128)(2,1)S(1)} %bitcast.27), channel_id=1, source_target_pairs={{0,32},{16,48},{32,64},{48,80},{64,96},{80,112},{96,0},{112,16},{1... | collective-permute-start | bytes 786440 | tf_op jit(solution)/shard_map/ppermute | solution.py:464
  161.7 10.9 %collective-permute-start.7 = (bf16[128,1024]{1,0:T(8,128)(2,1)S(1)}, bf16[128,1024]{1,0:T(8,128)(2,1)S(1)}, u32[]{:S(2)}, u32[]{:S(2)}) collective-permute-start(bf16[128,1024]{1,0:T(8,128)(2,1)S(1)} %bitcast.28), channel_id=1, source_target_pairs={{0,96},{16,112},{32,0},{48,16},{64,32},{80,48},{96,64},{112,80},{1... | collective-permute-start | bytes 786440 | tf_op jit(solution)/shard_map/ppermute | solution.py:465
  163.7 20.8 %collective-permute-start.10 = (bf16[128,1024]{1,0:T(8,128)(2,1)S(1)}, bf16[128,1024]{1,0:T(8,128)(2,1)S(1)}, u32[]{:S(2)}, u32[]{:S(2)}) collective-permute-start(bf16[128,1024]{1,0:T(8,128)(2,1)S(1)} %bitcast.29), channel_id=1, source_target_pairs={{0,16},{16,0},{32,48},{48,32},{64,80},{80,64},{96,112},{112,96},{1... | collective-permute-start | bytes 786440 | tf_op jit(solution)/shard_map/ppermute | solution.py:469
  172.5 7.7 %collective-permute-start.8 = (bf16[64,1024]{1,0:T(8,128)(2,1)S(1)}, bf16[64,1024]{1,0:T(8,128)(2,1)S(1)}, u32[]{:S(2)}, u32[]{:S(2)}) collective-permute-start(bf16[64,1024]{1,0:T(8,128)(2,1)S(1)} %slice.41), channel_id=1, source_target_pairs={{0,32},{16,48},{32,64},{48,80},{64,96},{80,112},{96,0},{112,16},{1... | collective-permute-start | bytes 393224 | tf_op jit(solution)/shard_map/ppermute | solution.py:466
  172.6 10.5 %collective-permute-start.9 = (bf16[64,1024]{1,0:T(8,128)(2,1)S(1)}, bf16[64,1024]{1,0:T(8,128)(2,1)S(1)}, u32[]{:S(2)}, u32[]{:S(2)}) collective-permute-start(bf16[64,1024]{1,0:T(8,128)(2,1)S(1)} %slice.42), channel_id=1, source_target_pairs={{0,96},{16,112},{32,0},{48,16},{64,32},{80,48},{96,64},{112,80},{1... | collective-permute-start | bytes 393224 | tf_op jit(solution)/shard_map/ppermute | solution.py:467
  175.3 9.2 %collective-permute-start.11 = (bf16[128,1024]{1,0:T(8,128)(2,1)S(1)}, bf16[128,1024]{1,0:T(8,128)(2,1)S(1)}, u32[]{:S(2)}, u32[]{:S(2)}) collective-permute-start(bf16[128,1024]{1,0:T(8,128)(2,1)S(1)} %collective-permute-done.6.refs_1_), channel_id=1, source_target_pairs={{0,16},{16,0},{32,48},{48,32},{64,80},{80,64},{96,112},{112,96},{1... | collective-permute-start | bytes 786440 | tf_op jit(solution)/shard_map/ppermute | solution.py:469
  180.2 4.3 %collective-permute-start.12 = (bf16[128,1024]{1,0:T(8,128)(2,1)S(1)}, bf16[128,1024]{1,0:T(8,128)(2,1)S(1)}, u32[]{:S(2)}, u32[]{:S(2)}) collective-permute-start(bf16[128,1024]{1,0:T(8,128)(2,1)S(1)} %collective-permute-done.7.refs_2_), channel_id=1, source_target_pairs={{0,16},{16,0},{32,48},{48,32},{64,80},{80,64},{96,112},{112,96},{1... | collective-permute-start | bytes 786440 | tf_op jit(solution)/shard_map/ppermute | solution.py:469
  180.3 4.3 %collective-permute-start.13 = (bf16[64,1024]{1,0:T(8,128)(2,1)S(1)}, bf16[64,1024]{1,0:T(8,128)(2,1)S(1)}, u32[]{:S(2)}, u32[]{:S(2)}) collective-permute-start(bf16[64,1024]{1,0:T(8,128)(2,1)S(1)} %collective-permute-done.8.refs_3_), channel_id=1, source_target_pairs={{0,16},{16,0},{32,48},{48,32},{64,80},{80,64},{96,112},{112,96},{1... | collective-permute-start | bytes 393224 | tf_op jit(solution)/shard_map/ppermute | solution.py:469
  183.1 1.4 collective-permute-start.14
  (12 other events, 81.7 us)
Sparse Core Ops, SparseCore 0:
  14.4 70.7 all-gather.2
  133.1 53.3 all-gather.4
Sparse Core Ops, SparseCore 1:
  83.9 40.4 reduce-scatter.1

commit v2 on v1

--- a/solution.py
+++ b/solution.py
@@ -14,13 +14,15 @@
 ID_BITS = 6
 LOW_LANE = 8
 COUNT_LANE = 16
-FINE_STEP = 512
+FINE_STEP = 1024
 MIDDLE_STEP = 512
 TOP_STEP = 512
 LEFT_STEP = 1024
 EXACT = 256
 SIDE = 4
 MOST_SHARES = 16
+COPY_CHUNKS = 8
+LEFT_PARTS = 4
 LONG = 1_000_000_000_000
 BOTH = ("grp", "sub")
 
@@ -36,6 +38,38 @@
 def spread(block, axes):
     copies = lax.axis_size(axes)
     return swap(jnp.broadcast_to(block[None], (copies,) + block.shape), axes)
+
+
+def copy_kernel(in_ref, out_ref, held, got, sent):
+    chunk = in_ref.shape[0] // COPY_CHUNKS
+    loads, stores = [], []
+    for i in range(COPY_CHUNKS):
+        here = pl.ds(i * chunk, chunk)
+        loads.append(pltpu.make_async_copy(in_ref.at[here], held.at[here], got.at[i]))
+        stores.append(pltpu.make_async_copy(held.at[here], out_ref.at[here], sent.at[i]))
+    for load in loads:
+        load.start()
+    for load, store in zip(loads, stores):
+        load.wait()
+        store.start()
+    for store in stores:
+        store.wait()
+
+
+def copied(array):
+    return pl.pallas_call(
+        copy_kernel,
+        out_shape=jax.ShapeDtypeStruct(array.shape, array.dtype),
+        in_specs=[pl.BlockSpec(memory_space=pl.ANY)],
+        out_specs=pl.BlockSpec(memory_space=pl.ANY),
+        scratch_shapes=[
+            pltpu.VMEM(array.shape, array.dtype),
+            pltpu.SemaphoreType.DMA((COPY_CHUNKS,)),
+            pltpu.SemaphoreType.DMA((COPY_CHUNKS,)),
+        ],
+        compiler_params=pltpu.CompilerParams(vmem_limit_bytes=60 * 1024 * 1024),
+        cost_estimate=pl.CostEstimate(flops=0, bytes_accessed=4 * array.size, transcendentals=0),
+    )(array)
 
 
 def ring(count, apart, turn):
@@ -175,7 +209,7 @@
                 pl.BlockSpec((MOST_SHARES, LANES), whole),
             ],
         ),
-        compiler_params=pltpu.CompilerParams(vmem_limit_bytes=24 * 1024 * 1024),
+        compiler_params=pltpu.CompilerParams(vmem_limit_bytes=60 * 1024 * 1024),
         cost_estimate=pl.CostEstimate(
             flops=4 * slots * LANES * feat_dim, bytes_accessed=2 * 1024 * 1024, transcendentals=0
         ),
@@ -189,12 +223,11 @@
     )
 
 
-def fine_step(step, got_ref, ids_ref, old_fine_ref, held):
+def fine_step(step, got, ids_ref, old_fine, held):
     first = pl.multiple_of(step * FINE_STEP, FINE_STEP)
     found = hits(FINE_STEP, first, ids_ref[...])
     members = jnp.sum(found.astype(jnp.float32), axis=1, keepdims=True)
-    totals = dot(found.astype(jnp.bfloat16), got_ref[...])
-    totals = totals + old_fine_ref[...].astype(jnp.float32)
+    totals = dot(found.astype(jnp.bfloat16), got) + old_fine.astype(jnp.float32)
     held[pl.ds(first, FINE_STEP), :] = (totals * (1.0 / (members + 1.0))).astype(jnp.bfloat16)
 
 
@@ -205,7 +238,7 @@
 
     @pl.when(step < fine_steps)
     def _():
-        fine_step(step, got_ref, ids_ref, old_fine_ref, held)
+        fine_step(step, got_ref[...], ids_ref, old_fine_ref[...], held)
 
     @pl.when(step == fine_steps)
     def _():
@@ -224,7 +257,7 @@
 
 def left_levels(got, ids, old_fine, parents, middle_count):
     fine_count, feat_dim = old_fine.shape
-    half = feat_dim // 2
+    half = feat_dim // LEFT_PARTS
     slots = got.shape[0]
     fine_steps = fine_count // FINE_STEP
 
@@ -284,12 +317,12 @@
     fine_steps = held.shape[0] // FINE_STEP
     middle_steps = scaled.shape[0] // MIDDLE_STEP
     top_rows = top_ref.shape[0]
-    half = held.shape[1]
+    half = left_ref.shape[1]
     store = pltpu.make_async_copy(held, fine_ref.at[:, half:], sent)
 
     @pl.when(step < fine_steps)
     def _():
-        fine_step(step, got_ref, ids_ref, old_fine_ref, held)
+        fine_step(step, got_ref[:, half:], ids_ref, old_fine_ref[:, half:], held)
 
     @pl.when(step == fine_steps)
     def _():
@@ -327,7 +360,8 @@
     which, got, ids, old_fine, parents, members, old_middle, top_parents, left, kept, top_count
 ):
     fine_count, feat_dim = old_fine.shape
-    half = feat_dim // 2
+    half = feat_dim // LEFT_PARTS
+    rest = feat_dim - half
     middle_count = old_middle.shape[0]
     share_rows = members.shape[1]
     slots = got.shape[0]
@@ -336,7 +370,7 @@
     top_steps = top_count // TOP_STEP
 
     def fine_at(i, s):
-        return (jnp.minimum(i, fine_steps - 1), 1)
+        return (jnp.minimum(i, fine_steps - 1), 0)
 
     def middle_at(i, s):
         return (jnp.clip(i - fine_steps, 0, middle_steps - 1), 0)
@@ -347,21 +381,21 @@
     def whole(i, s):
         return (0, 0)
 
-    flops = 2 * half * (fine_count * slots + middle_count * (fine_count + 2 * top_count))
+    flops = 2 * rest * (fine_count * slots + middle_count * (fine_count + 2 * top_count))
     return pl.pallas_call(
         right_kernel,
         out_shape=(
             jax.ShapeDtypeStruct((fine_count, feat_dim), jnp.bfloat16),
-            jax.ShapeDtypeStruct((middle_count, half), jnp.bfloat16),
+            jax.ShapeDtypeStruct((middle_count, rest), jnp.bfloat16),
             jax.ShapeDtypeStruct((top_count, feat_dim), jnp.float32),
         ),
         grid_spec=pltpu.PrefetchScalarGridSpec(
             num_scalar_prefetch=1,
             grid=(fine_steps + middle_steps + top_steps,),
             in_specs=[
-                pl.BlockSpec((slots, half), lambda i, s: (0, 1)),
+                pl.BlockSpec((slots, feat_dim), whole),
                 pl.BlockSpec((1, slots), whole),
-                pl.BlockSpec((FINE_STEP, half), fine_at),
+                pl.BlockSpec((FINE_STEP, feat_dim), fine_at),
                 pl.BlockSpec((1, fine_count), whole),
                 pl.BlockSpec(members.shape, whole),
                 pl.BlockSpec((share_rows, feat_dim), lambda i, s: (s[0], 0)),
@@ -371,11 +405,11 @@
             ],
             out_specs=[
                 pl.BlockSpec(memory_space=pl.ANY),
-                pl.BlockSpec((MIDDLE_STEP, half), middle_at),
+                pl.BlockSpec((MIDDLE_STEP, rest), middle_at),
                 pl.BlockSpec((TOP_STEP, feat_dim), top_at),
             ],
             scratch_shapes=[
-                pltpu.VMEM((fine_count, half), jnp.bfloat16),
+                pltpu.VMEM((fine_count, rest), jnp.bfloat16),
                 pltpu.VMEM((middle_count, feat_dim), jnp.bfloat16),
                 pltpu.SemaphoreType.DMA,
             ],
@@ -548,19 +582,21 @@
         top_count,
     )
 
-    shares = (group_width, share_rows, feat_dim // 2)
-    left = swap(left.reshape(shares), "sub")
+    left = swap(left.reshape(group_width, share_rows, -1), "sub")
     right, left = lax.optimization_barrier((right, left))
-    right = swap(right.reshape(shares), "sub")
+    right = swap(right.reshape(group_width, share_rows, -1), "sub")
     wide_fine = old_fine.astype(jnp.float32)
     fine_norms = jnp.sum(wide_fine * wide_fine, axis=1)[None, :]
     found = candidate_parts(which, all_rows, old_fine, fine_norms, group_width)
-    left, right, found = lax.optimization_barrier((left, right, found))
+    right, found = lax.optimization_barrier((right, found))
     share_totals = lax.dynamic_slice_in_dim(middle_members, share, 1).reshape(share_rows)
     old_share = lax.dynamic_slice_in_dim(old_middle, share * share_rows, share_rows)
-    sums = [jnp.sum(parts.astype(jnp.float32), axis=0) for parts in (left, right)]
-    new_share = level_update(jnp.concatenate(sums, axis=1), share_totals, old_share)
-    new_middle = lax.all_gather(new_share, "sub", axis=0, tiled=True)
+    left_share, right_share = [
+        level_update(jnp.sum(parts.astype(jnp.float32), axis=0), share_totals, olds)
+        for parts, olds in zip((left, right), jnp.split(old_share, [feat_dim // LEFT_PARTS], axis=1))
+    ]
+    new_share = jnp.concatenate([left_share, right_share], axis=1)
+    new_middle = copied(lax.all_gather(new_share, "sub", axis=0, tiled=True))
 
     top_block = lax.psum_scatter(top_part, "grp", scatter_dimension=0, tiled=True)
     top_pieces = top_block.reshape(group_width, top_rows, feat_dim)

time: 200 us -> 198 us (0.990)
  local copies, waits for them, and re-layouts: 17.6 us -> 10.1 us
  waiting for transfers between devices: 33.9 us -> 39.5 us
  starting transfers between devices: 62.1 us -> 57.1 us
  Pallas kernels: 45.8 us -> 49.6 us
    unnamed x30 -> x19, local copies, waits for them, and re-layouts: 13.4 us -> 4.96 us
    all_to_all x4, starting transfers between devices: 27.7 us -> 22.2 us  [swap(): return lax.all_to_all(blocks, axes, split_axis=0, concat_axis=0, tiled=True)]
    pallas_call x1, Pallas kernels: 9.44 us -> 5.63 us  [left_levels(): pl.pallas_call(left_kernel, out_shape=(jax.ShapeDtypeStruct((fine_count,...]
    pallas_call x0 -> x1, Pallas kernels: none -> 3.57 us  [copied(): pl.pallas_call(copy_kernel, out_shape=jax.ShapeDtypeStruct(array.shape, a...]
    ppermute x6, waiting for transfers between devices: 4.22 us -> 7.3 us  [per_device(): lax.ppermute(middle_members, 'sub', ring(group_width, apart, turn))]
    pallas_call x1, Pallas kernels: 17.2 us -> 19.8 us  [right_levels(): pl.pallas_call(right_kernel, out_shape=(jax.ShapeDtypeStruct((fine_count,...]
    all_to_all x4, waiting for transfers between devices: 29.6 us -> 32.1 us  [swap(): return lax.all_to_all(blocks, axes, split_axis=0, concat_axis=0, tiled=True)]
  transfers between devices with their start and end apart: 22 -> 22, of which waited for: 8 -> 6; matrix products, arithmetic and copies ran while one was open for 9% -> 10% of each run, Pallas kernels for 22% -> 21%
where the time goes in v2:
time: 198 us; the launch traced here: 197 us
  starting transfers between devices  57.1 us (29%)
  Pallas kernels  49.6 us (25%)
  waiting for transfers between devices  39.5 us (20%)
  between operations  15.8 us (8%)
  other arithmetic  14.5 us (7%)
  blocking collectives  10.6 us (5%)
  local copies, waits for them, and re-layouts  10.1 us (5%)
    all_to_all x4, waiting for transfers between devices, swap(): return lax.all_to_all(blocks, axes, split_axis=0, concat_axis=0, tiled=True)  32.1 us
    all_to_all x4, starting transfers between devices, swap(): return lax.all_to_all(blocks, axes, split_axis=0, concat_axis=0, tiled=True)  22.2 us
    pallas_call x1, Pallas kernels, right_levels(): pl.pallas_call(right_kernel, out_shape=(jax.ShapeDtypeStruct((fine_count,...  19.8 us
    ppermute x5, starting transfers between devices, all_blocks(): pieces += [lax.ppermute(piece, 'grp', across) for piece in pieces]  17.5 us
    pallas_call x1, Pallas kernels, candidate_parts(): pl.pallas_call(distance_kernel, out_shape=jax.ShapeDtypeStruct((groups, S...  14.7 us
    ppermute x6, starting transfers between devices, per_device(): lax.ppermute(middle_members, 'sub', ring(group_width, apart, turn))  11.6 us
    all_to_all x1, blocking collectives, swap(): return lax.all_to_all(blocks, axes, split_axis=0, concat_axis=0, tiled=True)  10.6 us
    ppermute x6, waiting for transfers between devices, per_device(): lax.ppermute(middle_members, 'sub', ring(group_width, apart, turn))  7.3 us
  transfers between devices with their start and end apart: 22, of which 6 were waited for; matrix products, arithmetic and copies ran while one was open for 10% of the time, Pallas kernels for 21%

profile of v2, /device:TPU:1, one launch (start us, length us, event | category | flops | bytes accessed | tf_op | source)
XLA Modules:
  0.0 197.2 jit_solution(4380746500123411010)
XLA Ops:
  8.7 3.8 %shard_map.111 = (bf16[512,1024]{1,0:T(8,128)(2,1)}, bf16[64,1280]{1,0:T(8,128)(2,1)}, f32[16,128]{1,0:T(8,128)}) custom-call(s32[3]{0:T(128)} %pad_add_fusion.share_ref, s32[1,64]{1,0:T(1,128)} %bitcast.44, bf16[64,1024]{1,0:T(8,128)(2,1)} %points_ref.1, s32[1,2048]{1,0:T(1,128)} %bitcast.42, s32[1,2048]{1,0:T(1,128)} %bitcast.39, s32[64,128]{1,0:T(8,128)} %candidates_ref.1), custom_call_target="tpu_custom_call" | custom-call | flops 268435456 | bytes 2097152 | tf_op jit(solution)/shard_map/pallas_call | solution.py:189
  12.5 2.5 %collective-permute-start = (f32[16,128]{1,0:T(8,128)}, f32[16,128]{1,0:T(8,128)S(1)}, u32[]{:S(2)}, u32[]{:S(2)}) collective-permute-start(f32[16,128]{1,0:T(8,128)} %get-tuple-element.19), channel_id=1, source_target_pairs={{0,1},{1,2},{2,3},{3,0},{4,5},{5,6},{6,7},{7,4},{8,9},{9,10},{10,1... | collective-permute-start | bytes 24584 | tf_op jit(solution)/shard_map/ppermute | solution.py:562
  15.1 3.3 %collective-permute-start.1 = (f32[16,128]{1,0:T(8,128)}, f32[16,128]{1,0:T(8,128)S(1)}, u32[]{:S(2)}, u32[]{:S(2)}) collective-permute-start(f32[16,128]{1,0:T(8,128)} %get-tuple-element.19), channel_id=1, source_target_pairs={{0,2},{1,3},{2,0},{3,1},{4,6},{5,7},{6,4},{7,5},{8,10},{9,11},{10,... | collective-permute-start | bytes 24584 | tf_op jit(solution)/shard_map/ppermute | solution.py:562
  19.1 2.3 %reshape.49 = bf16[128,4,1024]{2,1,0:T(4,128)(2,1)} reshape(bf16[512,1024]{1,0:T(8,128)(2,1)} %get-tuple-element.18) | data formatting | bytes 2097152 | tf_op jit(solution)/shard_map/reshape | solution.py:550
  21.4 8.5 %all-to-all-start = ((bf16[128,4,1024]{2,1,0:T(4,128)(2,1)}), bf16[128,4,1024]{2,1,0:T(4,128)(2,1)S(1)}, u32[]{:S(2)}, u32[]{:S(2)}) async-start(bf16[128,4,1024]{2,1,0:T(4,128)(2,1)} %reshape.49), calls=%async_computation | async-start | bytes 2097152 | tf_op jit(solution)/shard_map/all_to_all | solution.py:35
  29.9 3.1 %multiply_reduce_fusion = f32[2048]{0:T(1024)S(1)} fusion(bf16[2048,1024]{1,0:T(8,128)(2,1)} %fine_ref.1), kind=kLoop, calls=%fused_computation | loop fusion | flops 6289408 | bytes 4202496 | tf_op jit(solution)/shard_map/reduce_sum | solution.py:589
  34.5 2.4 %collective-permute-start.4 = (f32[16,128]{1,0:T(8,128)S(1)}, f32[16,128]{1,0:T(8,128)S(1)}, u32[]{:S(2)}, u32[]{:S(2)}) collective-permute-start(f32[16,128]{1,0:T(8,128)S(1)} %add_add_fusion.1), channel_id=1, source_target_pairs={{0,8},{1,9},{2,10},{3,11},{4,12},{5,13},{6,14},{7,15},{8,0},{9,1},... | collective-permute-start | bytes 24584 | tf_op jit(solution)/shard_map/ppermute | solution.py:562
  38.7 6.8 %collective-permute-done.3 = f32[16,128]{1,0:T(8,128)S(1)} collective-permute-done((f32[16,128]{1,0:T(8,128)S(1)}, f32[16,128]{1,0:T(8,128)S(1)}, u32[]{:S(2)}, u32[]{:S(2)}) %collective-permute-start.3) | collective-permute-done | bytes 8224 | tf_op jit(solution)/shard_map/ppermute | solution.py:562
  46.6 3.4 %all-to-all-done = bf16[128,4,1024]{2,1,0:T(4,128)(2,1)S(1)} async-done(((bf16[128,4,1024]{2,1,0:T(4,128)(2,1)}), bf16[128,4,1024]{2,1,0:T(4,128)(2,1)S(1)}, u32[]{:S(2)}, u32[]{:S(2)}) %all-to-all-start) | async-done | bytes 1048608 | tf_op jit(solution)/shard_map/all_to_all | solution.py:35
  52.6 5.6 %shard_map.112 = (bf16[2048,1024]{1,0:T(8,128)(2,1)}, bf16[2048,256]{1,0:T(8,128)(2,1)}) custom-call(bf16[512,1024]{1,0:T(8,128)(2,1)} %reshape.50.got_ref, s32[1,512]{1,0:T(1,128)} %reshape.51.ids_ref, bf16[2048,1024]{1,0:T(8,128)(2,1)} %fine_ref.1, s32[1,2048]{1,0:T(1,128)} %bitcast.40), custom_call_target="tpu_custom_call" | custom-call | flops 2684354560 | bytes 8388608 | tf_op jit(solution)/shard_map/pallas_call | solution.py:267
  58.2 3.7 %all-to-all-start.1 = ((bf16[16,128,256]{2,1,0:T(8,128)(2,1)}), bf16[16,128,256]{2,1,0:T(8,128)(2,1)S(1)}, u32[]{:S(2)}, u32[]{:S(2)}) async-start(bf16[16,128,256]{2,1,0:T(8,128)(2,1)} %bitcast.35), calls=%async_computation.1 | async-start | bytes 2097152 | tf_op jit(solution)/shard_map/all_to_all | solution.py:35
  61.9 19.8 %shard_map.113 = (bf16[2048,1024]{1,0:T(8,128)(2,1)}, bf16[2048,768]{1,0:T(8,128)(2,1)}, f32[1024,1024]{1,0:T(8,128)}) custom-call(s32[3]{0:T(128)} %pad_add_fusion.share_ref, bf16[512,1024]{1,0:T(8,128)(2,1)} %reshape.50.got_ref, s32[1,512]{1,0:T(1,128)} %reshape.51.ids_ref, bf16[2048,1024]{1,0:T(8,128)(2,1)} %fine_ref.1, ...), custom_call_target="tpu_custom_call", output_to_operand_aliasing={{0}: (9, {})} | custom-call | flops 14495514624 | bytes 14680064 | tf_op jit(solution)/shard_map/pallas_call | solution.py:385
  82.7 6.5 %all-to-all-start.2 = ((bf16[16,128,768]{2,1,0:T(8,128)(2,1)}), bf16[16,128,768]{2,1,0:T(8,128)(2,1)}, u32[]{:S(2)}, u32[]{:S(2)}) async-start(bf16[16,128,768]{2,1,0:T(8,128)(2,1)} %bitcast.32), calls=%async_computation.2 | async-start | bytes 6291456 | tf_op jit(solution)/shard_map/all_to_all | solution.py:35
  95.1 14.7 %shard_map.114 = f32[16,8,128]{2,1,0:T(8,128)S(1)} custom-call(s32[3]{0:T(128)S(1)} %copy-done.1, bf16[1024,1280]{1,0:T(8,128)(2,1)S(1)} %copy-done.2, bf16[2048,1024]{1,0:T(8,128)(2,1)S(1)} %copy-done, f32[1,2048]{1,0:T(1,128)S(1)} %bitcast.31), custom_call_target="tpu_custom_call" | custom-call | flops 999999995904 | bytes 6291456 | tf_op jit(solution)/shard_map/pallas_call | solution.py:461
  109.8 19.4 %all-to-all-done.2 = bf16[16,128,768]{2,1,0:T(8,128)(2,1)} async-done(((bf16[16,128,768]{2,1,0:T(8,128)(2,1)}), bf16[16,128,768]{2,1,0:T(8,128)(2,1)}, u32[]{:S(2)}, u32[]{:S(2)}) %all-to-all-start.2) | async-done | bytes 3145760 | tf_op jit(solution)/shard_map/all_to_all | solution.py:35
  129.2 2.4 %convert_reduce_fusion = f32[128,768]{1,0:T(8,128)S(1)} fusion(bf16[16,128,768]{2,1,0:T(8,128)(2,1)} %all-to-all-done.2), kind=kLoop, calls=%fused_computation.1 | loop fusion | flops 3047424 | bytes 3538944 | tf_op jit(solution)/shard_map/reduce_sum | solution.py:595
  135.3 3.6 %all-to-all-start.3 = ((f32[16,8,1152]{2,1,0:T(8,128)}), f32[16,8,1152]{2,1,0:T(8,128)S(1)}, u32[]{:S(2)}, u32[]{:S(2)}) async-start(f32[16,8,1152]{2,1,0:T(8,128)} %pad_maximum_fusion), calls=%async_computation.4 | async-start | bytes 1179648 | tf_op jit(solution)/shard_map/all_to_all | solution.py:35
  139.0 9.2 %all-to-all-done.3 = f32[16,8,1152]{2,1,0:T(8,128)S(1)} async-done(((f32[16,8,1152]{2,1,0:T(8,128)}), f32[16,8,1152]{2,1,0:T(8,128)S(1)}, u32[]{:S(2)}, u32[]{:S(2)}) %all-to-all-start.3) | async-done | bytes 589856 | tf_op jit(solution)/shard_map/all_to_all | solution.py:35
  149.1 10.6 %all_to_all.25 = bf16[16,8,1024]{2,1,0:T(8,128)(2,1)S(1)} all-to-all(bf16[16,8,1024]{2,1,0:T(8,128)(2,1)S(1)} %broadcast_in_dim.32), channel_id=1, replica_groups=mesh['grp'=8,'sub'=16] {'sub'}, dimensions={0} | all-to-all | bytes 524288 | tf_op jit(solution)/shard_map/all_to_all | solution.py:35
  162.4 9.7 %collective-permute-start.10 = (bf16[128,1024]{1,0:T(8,128)(2,1)S(1)}, bf16[128,1024]{1,0:T(8,128)(2,1)S(1)}, u32[]{:S(2)}, u32[]{:S(2)}) collective-permute-start(bf16[128,1024]{1,0:T(8,128)(2,1)S(1)} %bitcast.29), channel_id=1, source_target_pairs={{0,16},{16,0},{32,48},{48,32},{64,80},{80,64},{96,112},{112,96},{1... | collective-permute-start | bytes 786440 | tf_op jit(solution)/shard_map/ppermute | solution.py:503
  172.2 2.7 %collective-permute-start.9 = (bf16[64,1024]{1,0:T(8,128)(2,1)S(1)}, bf16[64,1024]{1,0:T(8,128)(2,1)S(1)}, u32[]{:S(2)}, u32[]{:S(2)}) collective-permute-start(bf16[64,1024]{1,0:T(8,128)(2,1)S(1)} %slice.42), channel_id=1, source_target_pairs={{0,96},{16,112},{32,0},{48,16},{64,32},{80,48},{96,64},{112,80},{1... | collective-permute-start | bytes 393224 | tf_op jit(solution)/shard_map/ppermute | solution.py:501
  174.9 4.9 %collective-permute-start.11 = (bf16[128,1024]{1,0:T(8,128)(2,1)S(1)}, bf16[128,1024]{1,0:T(8,128)(2,1)S(1)}, u32[]{:S(2)}, u32[]{:S(2)}) collective-permute-start(bf16[128,1024]{1,0:T(8,128)(2,1)S(1)} %collective-permute-done.6.refs_1_), channel_id=1, source_target_pairs={{0,16},{16,0},{32,48},{48,32},{64,80},{80,64},{96,112},{112,96},{1... | collective-permute-start | bytes 786440 | tf_op jit(solution)/shard_map/ppermute | solution.py:503
  179.8 2.8 %collective-permute-start.13 = (bf16[64,1024]{1,0:T(8,128)(2,1)S(1)}, bf16[64,1024]{1,0:T(8,128)(2,1)S(1)}, u32[]{:S(2)}, u32[]{:S(2)}) collective-permute-start(bf16[64,1024]{1,0:T(8,128)(2,1)S(1)} %collective-permute-done.8.refs_3_), channel_id=1, source_target_pairs={{0,16},{16,0},{32,48},{48,32},{64,80},{80,64},{96,112},{112,96},{1... | collective-permute-start | bytes 393224 | tf_op jit(solution)/shard_map/ppermute | solution.py:503
  186.1 3.6 %shard_map.115 = bf16[2048,1024]{1,0:T(8,128)(2,1)} custom-call(bf16[2048,1024]{1,0:T(8,128)(2,1)} %all-gather.5.cloned.1.call-done.in_ref), custom_call_target="tpu_custom_call" | custom-call | bytes 8388608 | tf_op jit(solution)/shard_map/pallas_call | solution.py:60
  (78 shorter events, 26.0 us)
Async XLA Ops:
  8.0 83.1 %all-gather.3.cloned.1.call-start = ((), (), s32[]{:S(2)}) async-start(), calls=%async_computation.6 | async-start | bytes 2785280 | tf_op jit(solution)/shard_map/all_gather | solution.py:558
  12.5 20.5 %collective-permute-start = (f32[16,128]{1,0:T(8,128)}, f32[16,128]{1,0:T(8,128)S(1)}, u32[]{:S(2)}, u32[]{:S(2)}) collective-permute-start(f32[16,128]{1,0:T(8,128)} %get-tuple-element.19), channel_id=1, source_target_pairs={{0,1},{1,2},{2,3},{3,0},{4,5},{5,6},{6,7},{7,4},{8,9},{9,10},{10,1... | collective-permute-start | bytes 24584 | tf_op jit(solution)/shard_map/ppermute | solution.py:562
  15.1 17.9 %collective-permute-start.1 = (f32[16,128]{1,0:T(8,128)}, f32[16,128]{1,0:T(8,128)S(1)}, u32[]{:S(2)}, u32[]{:S(2)}) collective-permute-start(f32[16,128]{1,0:T(8,128)} %get-tuple-element.19), channel_id=1, source_target_pairs={{0,2},{1,3},{2,0},{3,1},{4,6},{5,7},{6,4},{7,5},{8,10},{9,11},{10,... | collective-permute-start | bytes 24584 | tf_op jit(solution)/shard_map/ppermute | solution.py:562
  18.4 14.7 %collective-permute-start.2 = (f32[16,128]{1,0:T(8,128)}, f32[16,128]{1,0:T(8,128)S(1)}, u32[]{:S(2)}, u32[]{:S(2)}) collective-permute-start(f32[16,128]{1,0:T(8,128)} %get-tuple-element.19), channel_id=1, source_target_pairs={{0,3},{1,0},{2,1},{3,2},{4,7},{5,4},{6,5},{7,6},{8,11},{9,8},{10,9... | collective-permute-start | bytes 24584 | tf_op jit(solution)/shard_map/ppermute | solution.py:562
  21.4 28.6 %all-to-all-start = ((bf16[128,4,1024]{2,1,0:T(4,128)(2,1)}), bf16[128,4,1024]{2,1,0:T(4,128)(2,1)S(1)}, u32[]{:S(2)}, u32[]{:S(2)}) async-start(bf16[128,4,1024]{2,1,0:T(4,128)(2,1)} %reshape.49), calls=%async_computation | async-start | bytes 2097152 | tf_op jit(solution)/shard_map/all_to_all | solution.py:35
  33.1 12.5 %collective-permute-start.3 = (f32[16,128]{1,0:T(8,128)S(1)}, f32[16,128]{1,0:T(8,128)S(1)}, u32[]{:S(2)}, u32[]{:S(2)}) collective-permute-start(f32[16,128]{1,0:T(8,128)S(1)} %add_add_fusion.1), channel_id=1, source_target_pairs={{0,4},{1,5},{2,6},{3,7},{4,8},{5,9},{6,10},{7,11},{8,12},{9,13},{1... | collective-permute-start | bytes 24584 | tf_op jit(solution)/shard_map/ppermute | solution.py:562
  34.5 11.5 %collective-permute-start.4 = (f32[16,128]{1,0:T(8,128)S(1)}, f32[16,128]{1,0:T(8,128)S(1)}, u32[]{:S(2)}, u32[]{:S(2)}) collective-permute-start(f32[16,128]{1,0:T(8,128)S(1)} %add_add_fusion.1), channel_id=1, source_target_pairs={{0,8},{1,9},{2,10},{3,11},{4,12},{5,13},{6,14},{7,15},{8,0},{9,1},... | collective-permute-start | bytes 24584 | tf_op jit(solution)/shard_map/ppermute | solution.py:562
  36.9 9.1 %collective-permute-start.5 = (f32[16,128]{1,0:T(8,128)S(1)}, f32[16,128]{1,0:T(8,128)S(1)}, u32[]{:S(2)}, u32[]{:S(2)}) collective-permute-start(f32[16,128]{1,0:T(8,128)S(1)} %add_add_fusion.1), channel_id=1, source_target_pairs={{0,12},{1,13},{2,14},{3,15},{4,0},{5,1},{6,2},{7,3},{8,4},{9,5},{1... | collective-permute-start | bytes 24584 | tf_op jit(solution)/shard_map/ppermute | solution.py:562
  58.2 24.5 %all-to-all-start.1 = ((bf16[16,128,256]{2,1,0:T(8,128)(2,1)}), bf16[16,128,256]{2,1,0:T(8,128)(2,1)S(1)}, u32[]{:S(2)}, u32[]{:S(2)}) async-start(bf16[16,128,256]{2,1,0:T(8,128)(2,1)} %bitcast.35), calls=%async_computation.1 | async-start | bytes 2097152 | tf_op jit(solution)/shard_map/all_to_all | solution.py:35
  61.9 71.5 %reduce-scatter.2.cloned.1.call-start = ((), (), s32[]{:S(2)}) async-start(), calls=%async_computation.8 | async-start | bytes 4718592 | tf_op jit(solution)/shard_map/reduce_scatter | solution.py:601
  82.5 27.3 %copy-start.8 = (f32[128]{0:T(128)}, f32[128]{0:T(128)S(1)}, u32[]{:S(2)}) copy-start(f32[128]{0:T(128)S(1)} %fusion.3) | copy-start | bytes 1540
  82.7 46.5 %all-to-all-start.2 = ((bf16[16,128,768]{2,1,0:T(8,128)(2,1)}), bf16[16,128,768]{2,1,0:T(8,128)(2,1)}, u32[]{:S(2)}, u32[]{:S(2)}) async-start(bf16[16,128,768]{2,1,0:T(8,128)(2,1)} %bitcast.32), calls=%async_computation.2 | async-start | bytes 6291456 | tf_op jit(solution)/shard_map/all_to_all | solution.py:35
  89.2 96.9 %all-gather.5.cloned.1.call-start = ((), (), s32[]{:S(2)}) async-start(), calls=%async_computation.7 | async-start | bytes 4456448 | tf_op jit(solution)/shard_map/all_gather | solution.py:599
  109.8 29.1 %copy-start.4 = (f32[128,1,128]{2,1,0:T(1,128)S(1)}, f32[128,1,128]{2,1,0:T(1,128)}, u32[]{:S(2)}) copy-start(f32[128,1,128]{2,1,0:T(1,128)} %copy-done.3) | copy-start | bytes 196612
  135.3 12.9 %all-to-all-start.3 = ((f32[16,8,1152]{2,1,0:T(8,128)}), f32[16,8,1152]{2,1,0:T(8,128)S(1)}, u32[]{:S(2)}, u32[]{:S(2)}) async-start(f32[16,8,1152]{2,1,0:T(8,128)} %pad_maximum_fusion), calls=%async_computation.4 | async-start | bytes 1179648 | tf_op jit(solution)/shard_map/all_to_all | solution.py:35
  159.7 12.4 %collective-permute-start.6 = (bf16[128,1024]{1,0:T(8,128)(2,1)S(1)}, bf16[128,1024]{1,0:T(8,128)(2,1)S(1)}, u32[]{:S(2)}, u32[]{:S(2)}) collective-permute-start(bf16[128,1024]{1,0:T(8,128)(2,1)S(1)} %bitcast.27), channel_id=1, source_target_pairs={{0,32},{16,48},{32,64},{48,80},{64,96},{80,112},{96,0},{112,16},{1... | collective-permute-start | bytes 786440 | tf_op jit(solution)/shard_map/ppermute | solution.py:498
  160.3 11.8 %collective-permute-start.7 = (bf16[128,1024]{1,0:T(8,128)(2,1)S(1)}, bf16[128,1024]{1,0:T(8,128)(2,1)S(1)}, u32[]{:S(2)}, u32[]{:S(2)}) collective-permute-start(bf16[128,1024]{1,0:T(8,128)(2,1)S(1)} %bitcast.28), channel_id=1, source_target_pairs={{0,96},{16,112},{32,0},{48,16},{64,32},{80,48},{96,64},{112,80},{1... | collective-permute-start | bytes 786440 | tf_op jit(solution)/shard_map/ppermute | solution.py:499
  162.4 21.7 %collective-permute-start.10 = (bf16[128,1024]{1,0:T(8,128)(2,1)S(1)}, bf16[128,1024]{1,0:T(8,128)(2,1)S(1)}, u32[]{:S(2)}, u32[]{:S(2)}) collective-permute-start(bf16[128,1024]{1,0:T(8,128)(2,1)S(1)} %bitcast.29), channel_id=1, source_target_pairs={{0,16},{16,0},{32,48},{48,32},{64,80},{80,64},{96,112},{112,96},{1... | collective-permute-start | bytes 786440 | tf_op jit(solution)/shard_map/ppermute | solution.py:503
  172.1 7.7 %collective-permute-start.8 = (bf16[64,1024]{1,0:T(8,128)(2,1)S(1)}, bf16[64,1024]{1,0:T(8,128)(2,1)S(1)}, u32[]{:S(2)}, u32[]{:S(2)}) collective-permute-start(bf16[64,1024]{1,0:T(8,128)(2,1)S(1)} %slice.41), channel_id=1, source_target_pairs={{0,32},{16,48},{32,64},{48,80},{64,96},{80,112},{96,0},{112,16},{1... | collective-permute-start | bytes 393224 | tf_op jit(solution)/shard_map/ppermute | solution.py:500
  172.2 10.5 %collective-permute-start.9 = (bf16[64,1024]{1,0:T(8,128)(2,1)S(1)}, bf16[64,1024]{1,0:T(8,128)(2,1)S(1)}, u32[]{:S(2)}, u32[]{:S(2)}) collective-permute-start(bf16[64,1024]{1,0:T(8,128)(2,1)S(1)} %slice.42), channel_id=1, source_target_pairs={{0,96},{16,112},{32,0},{48,16},{64,32},{80,48},{96,64},{112,80},{1... | collective-permute-start | bytes 393224 | tf_op jit(solution)/shard_map/ppermute | solution.py:501
  174.9 9.2 %collective-permute-start.11 = (bf16[128,1024]{1,0:T(8,128)(2,1)S(1)}, bf16[128,1024]{1,0:T(8,128)(2,1)S(1)}, u32[]{:S(2)}, u32[]{:S(2)}) collective-permute-start(bf16[128,1024]{1,0:T(8,128)(2,1)S(1)} %collective-permute-done.6.refs_1_), channel_id=1, source_target_pairs={{0,16},{16,0},{32,48},{48,32},{64,80},{80,64},{96,112},{112,96},{1... | collective-permute-start | bytes 786440 | tf_op jit(solution)/shard_map/ppermute | solution.py:503
  179.8 4.3 %collective-permute-start.12 = (bf16[128,1024]{1,0:T(8,128)(2,1)S(1)}, bf16[128,1024]{1,0:T(8,128)(2,1)S(1)}, u32[]{:S(2)}, u32[]{:S(2)}) collective-permute-start(bf16[128,1024]{1,0:T(8,128)(2,1)S(1)} %collective-permute-done.7.refs_2_), channel_id=1, source_target_pairs={{0,16},{16,0},{32,48},{48,32},{64,80},{80,64},{96,112},{112,96},{1... | collective-permute-start | bytes 786440 | tf_op jit(solution)/shard_map/ppermute | solution.py:503
  179.8 4.3 %collective-permute-start.13 = (bf16[64,1024]{1,0:T(8,128)(2,1)S(1)}, bf16[64,1024]{1,0:T(8,128)(2,1)S(1)}, u32[]{:S(2)}, u32[]{:S(2)}) collective-permute-start(bf16[64,1024]{1,0:T(8,128)(2,1)S(1)} %collective-permute-done.8.refs_3_), channel_id=1, source_target_pairs={{0,16},{16,0},{32,48},{48,32},{64,80},{80,64},{96,112},{112,96},{1... | collective-permute-start | bytes 393224 | tf_op jit(solution)/shard_map/ppermute | solution.py:503
  182.7 1.4 collective-permute-start.14
  (7 other events, 69.6 us)
Sparse Core Ops, SparseCore 0:
  12.6 65.0 all-gather.2
  133.5 52.6 all-gather.4
Sparse Core Ops, SparseCore 1:
  81.9 35.5 reduce-scatter.1

commit v3 on v2

--- a/solution.py
+++ b/solution.py
@@ -22,7 +22,7 @@
 SIDE = 4
 MOST_SHARES = 16
 COPY_CHUNKS = 8
-LEFT_PARTS = 4
+LEFT_PARTS = 2
 LONG = 1_000_000_000_000
 BOTH = ("grp", "sub")
 

time: 198 us -> 196 us (0.990)
  waiting for transfers between devices: 39.5 us -> 32.6 us
  starting transfers between devices: 57.1 us -> 62.9 us
    all_to_all x4, starting transfers between devices: 22.2 us -> 28.1 us  [swap(): return lax.all_to_all(blocks, axes, split_axis=0, concat_axis=0, tiled=True)]
    all_to_all x4, waiting for transfers between devices: 32.1 us -> 28.4 us  [swap(): return lax.all_to_all(blocks, axes, split_axis=0, concat_axis=0, tiled=True)]
    ppermute x6, waiting for transfers between devices: 7.3 us -> 4.14 us  [per_device(): lax.ppermute(middle_members, 'sub', ring(group_width, apart, turn))]
    pallas_call x1, Pallas kernels: 5.63 us -> 8.75 us  [left_levels(): pl.pallas_call(left_kernel, out_shape=(jax.ShapeDtypeStruct((fine_count,...]
    pallas_call x1, Pallas kernels: 19.8 us -> 16.9 us  [right_levels(): pl.pallas_call(right_kernel, out_shape=(jax.ShapeDtypeStruct((fine_count,...]
  transfers between devices with their start and end apart: 22 -> 22, of which waited for: 6 -> 8; matrix products, arithmetic and copies ran while one was open for 10% -> 10% of each run, Pallas kernels for 21% -> 22%
where the time goes in v3:
time: 196 us; the launch traced here: 195 us
  starting transfers between devices  62.9 us (32%)
  Pallas kernels  49.8 us (25%)
  waiting for transfers between devices  32.6 us (17%)
  between operations  15.8 us (8%)
  other arithmetic  13.9 us (7%)
  blocking collectives  10.3 us (5%)
  local copies, waits for them, and re-layouts  10.2 us (5%)
    all_to_all x4, waiting for transfers between devices, swap(): return lax.all_to_all(blocks, axes, split_axis=0, concat_axis=0, tiled=True)  28.4 us
    all_to_all x4, starting transfers between devices, swap(): return lax.all_to_all(blocks, axes, split_axis=0, concat_axis=0, tiled=True)  28.1 us
    pallas_call x1, Pallas kernels, right_levels(): pl.pallas_call(right_kernel, out_shape=(jax.ShapeDtypeStruct((fine_count,...  16.9 us
    ppermute x5, starting transfers between devices, all_blocks(): pieces += [lax.ppermute(piece, 'grp', across) for piece in pieces]  16.5 us
    pallas_call x1, Pallas kernels, candidate_parts(): pl.pallas_call(distance_kernel, out_shape=jax.ShapeDtypeStruct((groups, S...  14.7 us
    ppermute x6, starting transfers between devices, per_device(): lax.ppermute(middle_members, 'sub', ring(group_width, apart, turn))  12.5 us
    all_to_all x1, blocking collectives, swap(): return lax.all_to_all(blocks, axes, split_axis=0, concat_axis=0, tiled=True)  10.3 us
    pallas_call x1, Pallas kernels, left_levels(): pl.pallas_call(left_kernel, out_shape=(jax.ShapeDtypeStruct((fine_count,...  8.75 us
  transfers between devices with their start and end apart: 22, of which 8 were waited for; matrix products, arithmetic and copies ran while one was open for 10% of the time, Pallas kernels for 22%

profile of v3, /device:TPU:1, one launch (start us, length us, event | category | flops | bytes accessed | tf_op | source)
XLA Modules:
  0.0 195.5 jit_solution(17412821920327913396)
XLA Ops:
  8.7 3.8 %shard_map.111 = (bf16[512,1024]{1,0:T(8,128)(2,1)}, bf16[64,1280]{1,0:T(8,128)(2,1)}, f32[16,128]{1,0:T(8,128)}) custom-call(s32[3]{0:T(128)} %pad_add_fusion.share_ref, s32[1,64]{1,0:T(1,128)} %bitcast.44, bf16[64,1024]{1,0:T(8,128)(2,1)} %points_ref.1, s32[1,2048]{1,0:T(1,128)} %bitcast.42, s32[1,2048]{1,0:T(1,128)} %bitcast.39, s32[64,128]{1,0:T(8,128)} %candidates_ref.1), custom_call_target="tpu_custom_call" | custom-call | flops 268435456 | bytes 2097152 | tf_op jit(solution)/shard_map/pallas_call | solution.py:189
  14.8 11.5 %all-to-all-start = ((bf16[128,4,1024]{2,1,0:T(4,128)(2,1)}), bf16[128,4,1024]{2,1,0:T(4,128)(2,1)S(1)}, u32[]{:S(2)}, u32[]{:S(2)}) async-start(bf16[128,4,1024]{2,1,0:T(4,128)(2,1)} %reshape.49), calls=%async_computation | async-start | bytes 2097152 | tf_op jit(solution)/shard_map/all_to_all | solution.py:35
  27.9 2.9 %collective-permute-start.1 = (f32[16,128]{1,0:T(8,128)S(1)}, f32[16,128]{1,0:T(8,128)S(1)}, u32[]{:S(2)}, u32[]{:S(2)}) collective-permute-start(f32[16,128]{1,0:T(8,128)S(1)} %copy-done.6), channel_id=1, source_target_pairs={{0,2},{1,3},{2,0},{3,1},{4,6},{5,7},{6,4},{7,5},{8,10},{9,11},{10,... | collective-permute-start | bytes 24584 | tf_op jit(solution)/shard_map/ppermute | solution.py:562
  31.8 2.6 %collective-permute-done.1 = f32[16,128]{1,0:T(8,128)S(1)} collective-permute-done((f32[16,128]{1,0:T(8,128)S(1)}, f32[16,128]{1,0:T(8,128)S(1)}, u32[]{:S(2)}, u32[]{:S(2)}) %collective-permute-start.1) | collective-permute-done | bytes 8224 | tf_op jit(solution)/shard_map/ppermute | solution.py:562
  35.0 2.5 %collective-permute-start.3 = (f32[16,128]{1,0:T(8,128)S(1)}, f32[16,128]{1,0:T(8,128)S(1)}, u32[]{:S(2)}, u32[]{:S(2)}) collective-permute-start(f32[16,128]{1,0:T(8,128)S(1)} %add_add_fusion.1), channel_id=1, source_target_pairs={{0,4},{1,5},{2,6},{3,7},{4,8},{5,9},{6,10},{7,11},{8,12},{9,13},{1... | collective-permute-start | bytes 24584 | tf_op jit(solution)/shard_map/ppermute | solution.py:562
  37.5 3.2 %collective-permute-start.4 = (f32[16,128]{1,0:T(8,128)S(1)}, f32[16,128]{1,0:T(8,128)S(1)}, u32[]{:S(2)}, u32[]{:S(2)}) collective-permute-start(f32[16,128]{1,0:T(8,128)S(1)} %add_add_fusion.1), channel_id=1, source_target_pairs={{0,8},{1,9},{2,10},{3,11},{4,12},{5,13},{6,14},{7,15},{8,0},{9,1},... | collective-permute-start | bytes 24584 | tf_op jit(solution)/shard_map/ppermute | solution.py:562
  44.2 3.0 %all-to-all-done = bf16[128,4,1024]{2,1,0:T(4,128)(2,1)S(1)} async-done(((bf16[128,4,1024]{2,1,0:T(4,128)(2,1)}), bf16[128,4,1024]{2,1,0:T(4,128)(2,1)S(1)}, u32[]{:S(2)}, u32[]{:S(2)}) %all-to-all-start) | async-done | bytes 1048608 | tf_op jit(solution)/shard_map/all_to_all | solution.py:35
  49.8 8.8 %shard_map.112 = (bf16[2048,1024]{1,0:T(8,128)(2,1)}, bf16[2048,512]{1,0:T(8,128)(2,1)}) custom-call(bf16[512,1024]{1,0:T(8,128)(2,1)} %reshape.50.got_ref, s32[1,512]{1,0:T(1,128)} %reshape.51.ids_ref, bf16[2048,1024]{1,0:T(8,128)(2,1)} %fine_ref.1, s32[1,2048]{1,0:T(1,128)} %bitcast.40), custom_call_target="tpu_custom_call" | custom-call | flops 5368709120 | bytes 8388608 | tf_op jit(solution)/shard_map/pallas_call | solution.py:267
  58.5 3.7 %all-to-all-start.1 = ((bf16[16,128,512]{2,1,0:T(8,128)(2,1)}), bf16[16,128,512]{2,1,0:T(8,128)(2,1)S(1)}, u32[]{:S(2)}, u32[]{:S(2)}) async-start(bf16[16,128,512]{2,1,0:T(8,128)(2,1)} %bitcast.33), calls=%async_computation.1 | async-start | bytes 4194304 | tf_op jit(solution)/shard_map/all_to_all | solution.py:35
  62.4 3.1 %multiply_reduce_fusion = f32[2048]{0:T(1024)S(1)} fusion(bf16[2048,1024]{1,0:T(8,128)(2,1)} %fine_ref.1), kind=kLoop, calls=%fused_computation | loop fusion | flops 6289408 | bytes 4202496 | tf_op jit(solution)/shard_map/reduce_sum | solution.py:589
  65.5 16.9 %shard_map.113 = (bf16[2048,1024]{1,0:T(8,128)(2,1)}, bf16[2048,512]{1,0:T(8,128)(2,1)}, f32[1024,1024]{1,0:T(8,128)}) custom-call(s32[3]{0:T(128)} %pad_add_fusion.share_ref, bf16[512,1024]{1,0:T(8,128)(2,1)} %reshape.50.got_ref, s32[1,512]{1,0:T(1,128)} %reshape.51.ids_ref, bf16[2048,1024]{1,0:T(8,128)(2,1)} %fine_ref.1, ...), custom_call_target="tpu_custom_call", output_to_operand_aliasing={{0}: (9, {})} | custom-call | flops 9663676416 | bytes 14680064 | tf_op jit(solution)/shard_map/pallas_call | solution.py:385
  83.7 10.5 %all-to-all-done.1 = bf16[16,128,512]{2,1,0:T(8,128)(2,1)S(1)} async-done(((bf16[16,128,512]{2,1,0:T(8,128)(2,1)}), bf16[16,128,512]{2,1,0:T(8,128)(2,1)S(1)}, u32[]{:S(2)}, u32[]{:S(2)}) %all-to-all-start.1) | async-done | bytes 2097184 | tf_op jit(solution)/shard_map/all_to_all | solution.py:35
  94.2 7.3 %all-to-all-start.2 = ((bf16[16,128,512]{2,1,0:T(8,128)(2,1)}), bf16[16,128,512]{2,1,0:T(8,128)(2,1)}, u32[]{:S(2)}, u32[]{:S(2)}) async-start(bf16[16,128,512]{2,1,0:T(8,128)(2,1)} %bitcast.34), calls=%async_computation.2 | async-start | bytes 4194304 | tf_op jit(solution)/shard_map/all_to_all | solution.py:35
  106.8 14.7 %shard_map.114 = f32[16,8,128]{2,1,0:T(8,128)S(1)} custom-call(s32[3]{0:T(128)S(1)} %copy-done.1, bf16[1024,1280]{1,0:T(8,128)(2,1)S(1)} %copy-done.2, bf16[2048,1024]{1,0:T(8,128)(2,1)S(1)} %copy-done, f32[1,2048]{1,0:T(1,128)S(1)} %bitcast.31), custom_call_target="tpu_custom_call" | custom-call | flops 999999995904 | bytes 6291456 | tf_op jit(solution)/shard_map/pallas_call | solution.py:461
  121.5 5.6 %all-to-all-done.2 = bf16[16,128,512]{2,1,0:T(8,128)(2,1)} async-done(((bf16[16,128,512]{2,1,0:T(8,128)(2,1)}), bf16[16,128,512]{2,1,0:T(8,128)(2,1)}, u32[]{:S(2)}, u32[]{:S(2)}) %all-to-all-start.2) | async-done | bytes 2097184 | tf_op jit(solution)/shard_map/all_to_all | solution.py:35
  132.8 5.5 %all-to-all-start.3 = ((f32[16,8,1152]{2,1,0:T(8,128)}), f32[16,8,1152]{2,1,0:T(8,128)S(1)}, u32[]{:S(2)}, u32[]{:S(2)}) async-start(f32[16,8,1152]{2,1,0:T(8,128)} %pad_maximum_fusion), calls=%async_computation.4 | async-start | bytes 1179648 | tf_op jit(solution)/shard_map/all_to_all | solution.py:35
  138.5 9.3 %all-to-all-done.3 = f32[16,8,1152]{2,1,0:T(8,128)S(1)} async-done(((f32[16,8,1152]{2,1,0:T(8,128)}), f32[16,8,1152]{2,1,0:T(8,128)S(1)}, u32[]{:S(2)}, u32[]{:S(2)}) %all-to-all-start.3) | async-done | bytes 589856 | tf_op jit(solution)/shard_map/all_to_all | solution.py:35
  148.6 10.3 %all_to_all.25 = bf16[16,8,1024]{2,1,0:T(8,128)(2,1)S(1)} all-to-all(bf16[16,8,1024]{2,1,0:T(8,128)(2,1)S(1)} %broadcast_in_dim.32), channel_id=1, replica_groups=mesh['grp'=8,'sub'=16] {'sub'}, dimensions={0} | all-to-all | bytes 524288 | tf_op jit(solution)/shard_map/all_to_all | solution.py:35
  158.9 2.7 %collective-permute-start.7 = (bf16[128,1024]{1,0:T(8,128)(2,1)S(1)}, bf16[128,1024]{1,0:T(8,128)(2,1)S(1)}, u32[]{:S(2)}, u32[]{:S(2)}) collective-permute-start(bf16[128,1024]{1,0:T(8,128)(2,1)S(1)} %bitcast.28), channel_id=1, source_target_pairs={{0,96},{16,112},{32,0},{48,16},{64,32},{80,48},{96,64},{112,80},{1... | collective-permute-start | bytes 786440 | tf_op jit(solution)/shard_map/ppermute | solution.py:499
  161.6 8.8 %collective-permute-start.10 = (bf16[128,1024]{1,0:T(8,128)(2,1)S(1)}, bf16[128,1024]{1,0:T(8,128)(2,1)S(1)}, u32[]{:S(2)}, u32[]{:S(2)}) collective-permute-start(bf16[128,1024]{1,0:T(8,128)(2,1)S(1)} %bitcast.29), channel_id=1, source_target_pairs={{0,16},{16,0},{32,48},{48,32},{64,80},{80,64},{96,112},{112,96},{1... | collective-permute-start | bytes 786440 | tf_op jit(solution)/shard_map/ppermute | solution.py:503
  170.5 2.7 %collective-permute-start.9 = (bf16[64,1024]{1,0:T(8,128)(2,1)S(1)}, bf16[64,1024]{1,0:T(8,128)(2,1)S(1)}, u32[]{:S(2)}, u32[]{:S(2)}) collective-permute-start(bf16[64,1024]{1,0:T(8,128)(2,1)S(1)} %slice.42), channel_id=1, source_target_pairs={{0,96},{16,112},{32,0},{48,16},{64,32},{80,48},{96,64},{112,80},{1... | collective-permute-start | bytes 393224 | tf_op jit(solution)/shard_map/ppermute | solution.py:501
  173.2 4.9 %collective-permute-start.11 = (bf16[128,1024]{1,0:T(8,128)(2,1)S(1)}, bf16[128,1024]{1,0:T(8,128)(2,1)S(1)}, u32[]{:S(2)}, u32[]{:S(2)}) collective-permute-start(bf16[128,1024]{1,0:T(8,128)(2,1)S(1)} %collective-permute-done.6.refs_1_), channel_id=1, source_target_pairs={{0,16},{16,0},{32,48},{48,32},{64,80},{80,64},{96,112},{112,96},{1... | collective-permute-start | bytes 786440 | tf_op jit(solution)/shard_map/ppermute | solution.py:503
  178.1 2.8 %collective-permute-start.13 = (bf16[64,1024]{1,0:T(8,128)(2,1)S(1)}, bf16[64,1024]{1,0:T(8,128)(2,1)S(1)}, u32[]{:S(2)}, u32[]{:S(2)}) collective-permute-start(bf16[64,1024]{1,0:T(8,128)(2,1)S(1)} %collective-permute-done.8.refs_3_), channel_id=1, source_target_pairs={{0,16},{16,0},{32,48},{48,32},{64,80},{80,64},{96,112},{112,96},{1... | collective-permute-start | bytes 393224 | tf_op jit(solution)/shard_map/ppermute | solution.py:503
  184.4 3.6 %shard_map.115 = bf16[2048,1024]{1,0:T(8,128)(2,1)} custom-call(bf16[2048,1024]{1,0:T(8,128)(2,1)} %all-gather.5.cloned.1.call-done.in_ref), custom_call_target="tpu_custom_call" | custom-call | bytes 8388608 | tf_op jit(solution)/shard_map/pallas_call | solution.py:60
  (77 shorter events, 29.0 us)
Async XLA Ops:
  8.0 34.1 %copy-start.7 = (s32[2048]{0:T(1024)S(1)}, s32[2048]{0:T(1024)}, u32[]{:S(2)}) copy-start(s32[2048]{0:T(1024)} %param.12) | copy-start | bytes 24580
  8.0 94.7 %all-gather.3.cloned.1.call-start = ((), (), s32[]{:S(2)}) async-start(), calls=%async_computation.6 | async-start | bytes 2785280 | tf_op jit(solution)/shard_map/all_gather | solution.py:558
  14.8 32.3 %all-to-all-start = ((bf16[128,4,1024]{2,1,0:T(4,128)(2,1)}), bf16[128,4,1024]{2,1,0:T(4,128)(2,1)S(1)}, u32[]{:S(2)}, u32[]{:S(2)}) async-start(bf16[128,4,1024]{2,1,0:T(4,128)(2,1)} %reshape.49), calls=%async_computation | async-start | bytes 2097152 | tf_op jit(solution)/shard_map/all_to_all | solution.py:35
  26.3 5.4 %collective-permute-start = (f32[16,128]{1,0:T(8,128)S(1)}, f32[16,128]{1,0:T(8,128)S(1)}, u32[]{:S(2)}, u32[]{:S(2)}) collective-permute-start(f32[16,128]{1,0:T(8,128)S(1)} %copy-done.6), channel_id=1, source_target_pairs={{0,1},{1,2},{2,3},{3,0},{4,5},{5,6},{6,7},{7,4},{8,9},{9,10},{10,1... | collective-permute-start | bytes 24584 | tf_op jit(solution)/shard_map/ppermute | solution.py:562
  27.9 6.4 %collective-permute-start.1 = (f32[16,128]{1,0:T(8,128)S(1)}, f32[16,128]{1,0:T(8,128)S(1)}, u32[]{:S(2)}, u32[]{:S(2)}) collective-permute-start(f32[16,128]{1,0:T(8,128)S(1)} %copy-done.6), channel_id=1, source_target_pairs={{0,2},{1,3},{2,0},{3,1},{4,6},{5,7},{6,4},{7,5},{8,10},{9,11},{10,... | collective-permute-start | bytes 24584 | tf_op jit(solution)/shard_map/ppermute | solution.py:562
  30.9 4.2 %collective-permute-start.2 = (f32[16,128]{1,0:T(8,128)S(1)}, f32[16,128]{1,0:T(8,128)S(1)}, u32[]{:S(2)}, u32[]{:S(2)}) collective-permute-start(f32[16,128]{1,0:T(8,128)S(1)} %copy-done.6), channel_id=1, source_target_pairs={{0,3},{1,0},{2,1},{3,2},{4,7},{5,4},{6,5},{7,6},{8,11},{9,8},{10,9... | collective-permute-start | bytes 24584 | tf_op jit(solution)/shard_map/ppermute | solution.py:562
  35.0 7.7 %collective-permute-start.3 = (f32[16,128]{1,0:T(8,128)S(1)}, f32[16,128]{1,0:T(8,128)S(1)}, u32[]{:S(2)}, u32[]{:S(2)}) collective-permute-start(f32[16,128]{1,0:T(8,128)S(1)} %add_add_fusion.1), channel_id=1, source_target_pairs={{0,4},{1,5},{2,6},{3,7},{4,8},{5,9},{6,10},{7,11},{8,12},{9,13},{1... | collective-permute-start | bytes 24584 | tf_op jit(solution)/shard_map/ppermute | solution.py:562
  37.5 5.7 %collective-permute-start.4 = (f32[16,128]{1,0:T(8,128)S(1)}, f32[16,128]{1,0:T(8,128)S(1)}, u32[]{:S(2)}, u32[]{:S(2)}) collective-permute-start(f32[16,128]{1,0:T(8,128)S(1)} %add_add_fusion.1), channel_id=1, source_target_pairs={{0,8},{1,9},{2,10},{3,11},{4,12},{5,13},{6,14},{7,15},{8,0},{9,1},... | collective-permute-start | bytes 24584 | tf_op jit(solution)/shard_map/ppermute | solution.py:562
  40.7 2.9 %collective-permute-start.5 = (f32[16,128]{1,0:T(8,128)S(1)}, f32[16,128]{1,0:T(8,128)S(1)}, u32[]{:S(2)}, u32[]{:S(2)}) collective-permute-start(f32[16,128]{1,0:T(8,128)S(1)} %add_add_fusion.1), channel_id=1, source_target_pairs={{0,12},{1,13},{2,14},{3,15},{4,0},{5,1},{6,2},{7,3},{8,4},{9,5},{1... | collective-permute-start | bytes 24584 | tf_op jit(solution)/shard_map/ppermute | solution.py:562
  58.5 35.6 %all-to-all-start.1 = ((bf16[16,128,512]{2,1,0:T(8,128)(2,1)}), bf16[16,128,512]{2,1,0:T(8,128)(2,1)S(1)}, u32[]{:S(2)}, u32[]{:S(2)}) async-start(bf16[16,128,512]{2,1,0:T(8,128)(2,1)} %bitcast.33), calls=%async_computation.1 | async-start | bytes 4194304 | tf_op jit(solution)/shard_map/all_to_all | solution.py:35
  62.3 68.6 %reduce-scatter.2.cloned.1.call-start = ((), (), s32[]{:S(2)}) async-start(), calls=%async_computation.8 | async-start | bytes 4718592 | tf_op jit(solution)/shard_map/reduce_scatter | solution.py:601
  94.2 32.9 %all-to-all-start.2 = ((bf16[16,128,512]{2,1,0:T(8,128)(2,1)}), bf16[16,128,512]{2,1,0:T(8,128)(2,1)}, u32[]{:S(2)}, u32[]{:S(2)}) async-start(bf16[16,128,512]{2,1,0:T(8,128)(2,1)} %bitcast.34), calls=%async_computation.2 | async-start | bytes 4194304 | tf_op jit(solution)/shard_map/all_to_all | solution.py:35
  101.5 83.0 %all-gather.5.cloned.1.call-start = ((), (), s32[]{:S(2)}) async-start(), calls=%async_computation.7 | async-start | bytes 4456448 | tf_op jit(solution)/shard_map/all_gather | solution.py:599
  106.8 22.2 %copy-start.8 = (f32[128]{0:T(128)S(1)}, f32[128]{0:T(128)}, u32[]{:S(2)}) copy-start(f32[128]{0:T(128)} %fusion.3) | copy-start | bytes 1540
  132.8 14.9 %all-to-all-start.3 = ((f32[16,8,1152]{2,1,0:T(8,128)}), f32[16,8,1152]{2,1,0:T(8,128)S(1)}, u32[]{:S(2)}, u32[]{:S(2)}) async-start(f32[16,8,1152]{2,1,0:T(8,128)} %pad_maximum_fusion), calls=%async_computation.4 | async-start | bytes 1179648 | tf_op jit(solution)/shard_map/all_to_all | solution.py:35
  158.9 11.5 %collective-permute-start.6 = (bf16[128,1024]{1,0:T(8,128)(2,1)S(1)}, bf16[128,1024]{1,0:T(8,128)(2,1)S(1)}, u32[]{:S(2)}, u32[]{:S(2)}) collective-permute-start(bf16[128,1024]{1,0:T(8,128)(2,1)S(1)} %bitcast.27), channel_id=1, source_target_pairs={{0,32},{16,48},{32,64},{48,80},{64,96},{80,112},{96,0},{112,16},{1... | collective-permute-start | bytes 786440 | tf_op jit(solution)/shard_map/ppermute | solution.py:498
  158.9 11.6 %collective-permute-start.7 = (bf16[128,1024]{1,0:T(8,128)(2,1)S(1)}, bf16[128,1024]{1,0:T(8,128)(2,1)S(1)}, u32[]{:S(2)}, u32[]{:S(2)}) collective-permute-start(bf16[128,1024]{1,0:T(8,128)(2,1)S(1)} %bitcast.28), channel_id=1, source_target_pairs={{0,96},{16,112},{32,0},{48,16},{64,32},{80,48},{96,64},{112,80},{1... | collective-permute-start | bytes 786440 | tf_op jit(solution)/shard_map/ppermute | solution.py:499
  161.6 20.8 %collective-permute-start.10 = (bf16[128,1024]{1,0:T(8,128)(2,1)S(1)}, bf16[128,1024]{1,0:T(8,128)(2,1)S(1)}, u32[]{:S(2)}, u32[]{:S(2)}) collective-permute-start(bf16[128,1024]{1,0:T(8,128)(2,1)S(1)} %bitcast.29), channel_id=1, source_target_pairs={{0,16},{16,0},{32,48},{48,32},{64,80},{80,64},{96,112},{112,96},{1... | collective-permute-start | bytes 786440 | tf_op jit(solution)/shard_map/ppermute | solution.py:503
  170.4 7.7 %collective-permute-start.8 = (bf16[64,1024]{1,0:T(8,128)(2,1)S(1)}, bf16[64,1024]{1,0:T(8,128)(2,1)S(1)}, u32[]{:S(2)}, u32[]{:S(2)}) collective-permute-start(bf16[64,1024]{1,0:T(8,128)(2,1)S(1)} %slice.41), channel_id=1, source_target_pairs={{0,32},{16,48},{32,64},{48,80},{64,96},{80,112},{96,0},{112,16},{1... | collective-permute-start | bytes 393224 | tf_op jit(solution)/shard_map/ppermute | solution.py:500
  170.5 10.5 %collective-permute-start.9 = (bf16[64,1024]{1,0:T(8,128)(2,1)S(1)}, bf16[64,1024]{1,0:T(8,128)(2,1)S(1)}, u32[]{:S(2)}, u32[]{:S(2)}) collective-permute-start(bf16[64,1024]{1,0:T(8,128)(2,1)S(1)} %slice.42), channel_id=1, source_target_pairs={{0,96},{16,112},{32,0},{48,16},{64,32},{80,48},{96,64},{112,80},{1... | collective-permute-start | bytes 393224 | tf_op jit(solution)/shard_map/ppermute | solution.py:501
  173.2 9.2 %collective-permute-start.11 = (bf16[128,1024]{1,0:T(8,128)(2,1)S(1)}, bf16[128,1024]{1,0:T(8,128)(2,1)S(1)}, u32[]{:S(2)}, u32[]{:S(2)}) collective-permute-start(bf16[128,1024]{1,0:T(8,128)(2,1)S(1)} %collective-permute-done.6.refs_1_), channel_id=1, source_target_pairs={{0,16},{16,0},{32,48},{48,32},{64,80},{80,64},{96,112},{112,96},{1... | collective-permute-start | bytes 786440 | tf_op jit(solution)/shard_map/ppermute | solution.py:503
  178.1 4.3 %collective-permute-start.12 = (bf16[128,1024]{1,0:T(8,128)(2,1)S(1)}, bf16[128,1024]{1,0:T(8,128)(2,1)S(1)}, u32[]{:S(2)}, u32[]{:S(2)}) collective-permute-start(bf16[128,1024]{1,0:T(8,128)(2,1)S(1)} %collective-permute-done.7.refs_2_), channel_id=1, source_target_pairs={{0,16},{16,0},{32,48},{48,32},{64,80},{80,64},{96,112},{112,96},{1... | collective-permute-start | bytes 786440 | tf_op jit(solution)/shard_map/ppermute | solution.py:503
  178.1 4.3 %collective-permute-start.13 = (bf16[64,1024]{1,0:T(8,128)(2,1)S(1)}, bf16[64,1024]{1,0:T(8,128)(2,1)S(1)}, u32[]{:S(2)}, u32[]{:S(2)}) collective-permute-start(bf16[64,1024]{1,0:T(8,128)(2,1)S(1)} %collective-permute-done.8.refs_3_), channel_id=1, source_target_pairs={{0,16},{16,0},{32,48},{48,32},{64,80},{80,64},{96,112},{112,96},{1... | collective-permute-start | bytes 393224 | tf_op jit(solution)/shard_map/ppermute | solution.py:503
  181.0 1.4 collective-permute-start.14
  (7 other events, 77.8 us)
Sparse Core Ops, SparseCore 0:
  12.7 68.6 all-gather.2
  131.0 53.2 all-gather.4
Sparse Core Ops, SparseCore 1:
  82.5 39.9 reduce-scatter.1

commit v4 on v3

--- a/solution.py
+++ b/solution.py
@@ -21,8 +21,8 @@
 EXACT = 256
 SIDE = 4
 MOST_SHARES = 16
-COPY_CHUNKS = 8
-LEFT_PARTS = 2
+COPY_CHUNKS = 16
+LEFT_EIGHTHS = 3
 LONG = 1_000_000_000_000
 BOTH = ("grp", "sub")
 
@@ -257,7 +257,7 @@
 
 def left_levels(got, ids, old_fine, parents, middle_count):
     fine_count, feat_dim = old_fine.shape
-    half = feat_dim // LEFT_PARTS
+    half = feat_dim // 8 * LEFT_EIGHTHS
     slots = got.shape[0]
     fine_steps = fine_count // FINE_STEP
 
@@ -360,7 +360,7 @@
     which, got, ids, old_fine, parents, members, old_middle, top_parents, left, kept, top_count
 ):
     fine_count, feat_dim = old_fine.shape
-    half = feat_dim // LEFT_PARTS
+    half = feat_dim // 8 * LEFT_EIGHTHS
     rest = feat_dim - half
     middle_count = old_middle.shape[0]
     share_rows = members.shape[1]
@@ -593,7 +593,7 @@
     old_share = lax.dynamic_slice_in_dim(old_middle, share * share_rows, share_rows)
     left_share, right_share = [
         level_update(jnp.sum(parts.astype(jnp.float32), axis=0), share_totals, olds)
-        for parts, olds in zip((left, right), jnp.split(old_share, [feat_dim // LEFT_PARTS], axis=1))
+        for parts, olds in zip((left, right), jnp.split(old_share, [feat_dim // 8 * LEFT_EIGHTHS], axis=1))
     ]
     new_share = jnp.concatenate([left_share, right_share], axis=1)
     new_middle = copied(lax.all_gather(new_share, "sub", axis=0, tiled=True))

time: 196 us -> 198 us (1.010)
  Pallas kernels: 49.8 us -> 52.7 us
  starting transfers between devices: 62.9 us -> 60.1 us
    pallas_call x1, Pallas kernels: 16.9 us -> 19.9 us  [right_levels(): pl.pallas_call(right_kernel, out_shape=(jax.ShapeDtypeStruct((fine_count,...]
    all_gather x1, waiting for transfers between devices: 0.01 us -> 2.76 us  [per_device(): new_middle = copied(lax.all_gather(new_share, 'sub', axis=0, tiled=True))]
    all_to_all x4, starting transfers between devices: 28.1 us -> 25.8 us  [swap(): return lax.all_to_all(blocks, axes, split_axis=0, concat_axis=0, tiled=True)]
    all_to_all x4, waiting for transfers between devices: 28.4 us -> 26.1 us  [swap(): return lax.all_to_all(blocks, axes, split_axis=0, concat_axis=0, tiled=True)]
    ppermute x1, starting transfers between devices: 0.01 us -> 2.05 us  [all_blocks(): before = lax.ppermute(block, 'grp', onward)]
  transfers between devices with their start and end apart: 22 -> 22, of which waited for: 8 -> 9; matrix products, arithmetic and copies ran while one was open for 10% -> 10% of each run, Pallas kernels for 22% -> 23%
where the time goes in v4:
time: 198 us; the launch traced here: 197 us
  starting transfers between devices  60.1 us (30%)
  Pallas kernels  52.7 us (27%)
  waiting for transfers between devices  33.1 us (17%)
  between operations  15.8 us (8%)
  other arithmetic  14.4 us (7%)
  blocking collectives  10.5 us (5%)
  local copies, waits for them, and re-layouts  10.3 us (5%)
    all_to_all x4, waiting for transfers between devices, swap(): return lax.all_to_all(blocks, axes, split_axis=0, concat_axis=0, tiled=True)  26.1 us
    all_to_all x4, starting transfers between devices, swap(): return lax.all_to_all(blocks, axes, split_axis=0, concat_axis=0, tiled=True)  25.8 us
    pallas_call x1, Pallas kernels, right_levels(): pl.pallas_call(right_kernel, out_shape=(jax.ShapeDtypeStruct((fine_count,...  19.9 us
    ppermute x5, starting transfers between devices, all_blocks(): pieces += [lax.ppermute(piece, 'grp', across) for piece in pieces]  15.3 us
    pallas_call x1, Pallas kernels, candidate_parts(): pl.pallas_call(distance_kernel, out_shape=jax.ShapeDtypeStruct((groups, S...  14.7 us
    ppermute x6, starting transfers between devices, per_device(): lax.ppermute(middle_members, 'sub', ring(group_width, apart, turn))  12.5 us
    all_to_all x1, blocking collectives, swap(): return lax.all_to_all(blocks, axes, split_axis=0, concat_axis=0, tiled=True)  10.5 us
    pallas_call x1, Pallas kernels, left_levels(): pl.pallas_call(left_kernel, out_shape=(jax.ShapeDtypeStruct((fine_count,...  8.43 us
  transfers between devices with their start and end apart: 22, of which 9 were waited for; matrix products, arithmetic and copies ran while one was open for 10% of the time, Pallas kernels for 23%

profile of v4, /device:TPU:1, one launch (start us, length us, event | category | flops | bytes accessed | tf_op | source)
XLA Modules:
  0.0 196.9 jit_solution(12011261689637931771)
XLA Ops:
  8.6 3.8 %shard_map.111 = (bf16[512,1024]{1,0:T(8,128)(2,1)}, bf16[64,1280]{1,0:T(8,128)(2,1)}, f32[16,128]{1,0:T(8,128)}) custom-call(s32[3]{0:T(128)} %pad_add_fusion.share_ref, s32[1,64]{1,0:T(1,128)} %bitcast.44, bf16[64,1024]{1,0:T(8,128)(2,1)} %points_ref.1, s32[1,2048]{1,0:T(1,128)} %bitcast.42, s32[1,2048]{1,0:T(1,128)} %bitcast.39, s32[64,128]{1,0:T(8,128)} %candidates_ref.1), custom_call_target="tpu_custom_call" | custom-call | flops 268435456 | bytes 2097152 | tf_op jit(solution)/shard_map/pallas_call | solution.py:189
  14.7 11.5 %all-to-all-start = ((bf16[128,4,1024]{2,1,0:T(4,128)(2,1)}), bf16[128,4,1024]{2,1,0:T(4,128)(2,1)S(1)}, u32[]{:S(2)}, u32[]{:S(2)}) async-start(bf16[128,4,1024]{2,1,0:T(4,128)(2,1)} %reshape.49), calls=%async_computation | async-start | bytes 2097152 | tf_op jit(solution)/shard_map/all_to_all | solution.py:35
  27.8 2.9 %collective-permute-start.1 = (f32[16,128]{1,0:T(8,128)S(1)}, f32[16,128]{1,0:T(8,128)S(1)}, u32[]{:S(2)}, u32[]{:S(2)}) collective-permute-start(f32[16,128]{1,0:T(8,128)S(1)} %copy-done.6), channel_id=1, source_target_pairs={{0,2},{1,3},{2,0},{3,1},{4,6},{5,7},{6,4},{7,5},{8,10},{9,11},{10,... | collective-permute-start | bytes 24584 | tf_op jit(solution)/shard_map/ppermute | solution.py:562
  31.7 2.6 %collective-permute-done.1 = f32[16,128]{1,0:T(8,128)S(1)} collective-permute-done((f32[16,128]{1,0:T(8,128)S(1)}, f32[16,128]{1,0:T(8,128)S(1)}, u32[]{:S(2)}, u32[]{:S(2)}) %collective-permute-start.1) | collective-permute-done | bytes 8224 | tf_op jit(solution)/shard_map/ppermute | solution.py:562
  35.0 2.5 %collective-permute-start.3 = (f32[16,128]{1,0:T(8,128)S(1)}, f32[16,128]{1,0:T(8,128)S(1)}, u32[]{:S(2)}, u32[]{:S(2)}) collective-permute-start(f32[16,128]{1,0:T(8,128)S(1)} %add_add_fusion.1), channel_id=1, source_target_pairs={{0,4},{1,5},{2,6},{3,7},{4,8},{5,9},{6,10},{7,11},{8,12},{9,13},{1... | collective-permute-start | bytes 24584 | tf_op jit(solution)/shard_map/ppermute | solution.py:562
  37.4 3.2 %collective-permute-start.4 = (f32[16,128]{1,0:T(8,128)S(1)}, f32[16,128]{1,0:T(8,128)S(1)}, u32[]{:S(2)}, u32[]{:S(2)}) collective-permute-start(f32[16,128]{1,0:T(8,128)S(1)} %add_add_fusion.1), channel_id=1, source_target_pairs={{0,8},{1,9},{2,10},{3,11},{4,12},{5,13},{6,14},{7,15},{8,0},{9,1},... | collective-permute-start | bytes 24584 | tf_op jit(solution)/shard_map/ppermute | solution.py:562
  44.1 3.0 %all-to-all-done = bf16[128,4,1024]{2,1,0:T(4,128)(2,1)S(1)} async-done(((bf16[128,4,1024]{2,1,0:T(4,128)(2,1)}), bf16[128,4,1024]{2,1,0:T(4,128)(2,1)S(1)}, u32[]{:S(2)}, u32[]{:S(2)}) %all-to-all-start) | async-done | bytes 1048608 | tf_op jit(solution)/shard_map/all_to_all | solution.py:35
  49.7 8.4 %shard_map.112 = (bf16[2048,1024]{1,0:T(8,128)(2,1)}, bf16[2048,384]{1,0:T(8,128)(2,1)}) custom-call(bf16[512,1024]{1,0:T(8,128)(2,1)} %reshape.50.got_ref, s32[1,512]{1,0:T(1,128)} %reshape.51.ids_ref, bf16[2048,1024]{1,0:T(8,128)(2,1)} %fine_ref.1, s32[1,2048]{1,0:T(1,128)} %bitcast.40), custom_call_target="tpu_custom_call" | custom-call | flops 4026531840 | bytes 8388608 | tf_op jit(solution)/shard_map/pallas_call | solution.py:267
  58.1 3.7 %all-to-all-start.1 = ((bf16[16,128,384]{2,1,0:T(8,128)(2,1)}), bf16[16,128,384]{2,1,0:T(8,128)(2,1)S(1)}, u32[]{:S(2)}, u32[]{:S(2)}) async-start(bf16[16,128,384]{2,1,0:T(8,128)(2,1)} %bitcast.34), calls=%async_computation.1 | async-start | bytes 3145728 | tf_op jit(solution)/shard_map/all_to_all | solution.py:35
  61.9 3.1 %multiply_reduce_fusion = f32[2048]{0:T(1024)S(1)} fusion(bf16[2048,1024]{1,0:T(8,128)(2,1)} %fine_ref.1), kind=kLoop, calls=%fused_computation | loop fusion | flops 6289408 | bytes 4202496 | tf_op jit(solution)/shard_map/reduce_sum | solution.py:589
  65.1 19.9 %shard_map.113 = (bf16[2048,1024]{1,0:T(8,128)(2,1)}, bf16[2048,640]{1,0:T(8,128)(2,1)}, f32[1024,1024]{1,0:T(8,128)}) custom-call(s32[3]{0:T(128)} %pad_add_fusion.share_ref, bf16[512,1024]{1,0:T(8,128)(2,1)} %reshape.50.got_ref, s32[1,512]{1,0:T(1,128)} %reshape.51.ids_ref, bf16[2048,1024]{1,0:T(8,128)(2,1)} %fine_ref.1, ...), custom_call_target="tpu_custom_call", output_to_operand_aliasing={{0}: (9, {})} | custom-call | flops 12079595520 | bytes 14680064 | tf_op jit(solution)/shard_map/pallas_call | solution.py:385
  85.7 3.1 %all-to-all-done.1 = bf16[16,128,384]{2,1,0:T(8,128)(2,1)S(1)} async-done(((bf16[16,128,384]{2,1,0:T(8,128)(2,1)}), bf16[16,128,384]{2,1,0:T(8,128)(2,1)S(1)}, u32[]{:S(2)}, u32[]{:S(2)}) %all-to-all-start.1) | async-done | bytes 1572896 | tf_op jit(solution)/shard_map/all_to_all | solution.py:35
  88.8 4.8 %all-to-all-start.2 = ((bf16[16,128,640]{2,1,0:T(8,128)(2,1)}), bf16[16,128,640]{2,1,0:T(8,128)(2,1)}, u32[]{:S(2)}, u32[]{:S(2)}) async-start(bf16[16,128,640]{2,1,0:T(8,128)(2,1)} %bitcast.32), calls=%async_computation.2 | async-start | bytes 5242880 | tf_op jit(solution)/shard_map/all_to_all | solution.py:35
  99.7 14.7 %shard_map.114 = f32[16,8,128]{2,1,0:T(8,128)S(1)} custom-call(s32[3]{0:T(128)S(1)} %copy-done.1, bf16[1024,1280]{1,0:T(8,128)(2,1)S(1)} %copy-done.2, bf16[2048,1024]{1,0:T(8,128)(2,1)S(1)} %copy-done, f32[1,2048]{1,0:T(1,128)S(1)} %bitcast.31), custom_call_target="tpu_custom_call" | custom-call | flops 999999995904 | bytes 6291456 | tf_op jit(solution)/shard_map/pallas_call | solution.py:461
  114.4 10.8 %all-to-all-done.2 = bf16[16,128,640]{2,1,0:T(8,128)(2,1)} async-done(((bf16[16,128,640]{2,1,0:T(8,128)(2,1)}), bf16[16,128,640]{2,1,0:T(8,128)(2,1)}, u32[]{:S(2)}, u32[]{:S(2)}) %all-to-all-start.2) | async-done | bytes 2621472 | tf_op jit(solution)/shard_map/all_to_all | solution.py:35
  131.1 5.8 %all-to-all-start.3 = ((f32[16,8,1152]{2,1,0:T(8,128)}), f32[16,8,1152]{2,1,0:T(8,128)S(1)}, u32[]{:S(2)}, u32[]{:S(2)}) async-start(f32[16,8,1152]{2,1,0:T(8,128)} %pad_maximum_fusion), calls=%async_computation.4 | async-start | bytes 1179648 | tf_op jit(solution)/shard_map/all_to_all | solution.py:35
  137.0 9.2 %all-to-all-done.3 = f32[16,8,1152]{2,1,0:T(8,128)S(1)} async-done(((f32[16,8,1152]{2,1,0:T(8,128)}), f32[16,8,1152]{2,1,0:T(8,128)S(1)}, u32[]{:S(2)}, u32[]{:S(2)}) %all-to-all-start.3) | async-done | bytes 589856 | tf_op jit(solution)/shard_map/all_to_all | solution.py:35
  147.1 10.5 %all_to_all.25 = bf16[16,8,1024]{2,1,0:T(8,128)(2,1)S(1)} all-to-all(bf16[16,8,1024]{2,1,0:T(8,128)(2,1)S(1)} %broadcast_in_dim.32), channel_id=1, replica_groups=mesh['grp'=8,'sub'=16] {'sub'}, dimensions={0} | all-to-all | bytes 524288 | tf_op jit(solution)/shard_map/all_to_all | solution.py:35
  161.2 7.6 %collective-permute-start.10 = (bf16[128,1024]{1,0:T(8,128)(2,1)S(1)}, bf16[128,1024]{1,0:T(8,128)(2,1)S(1)}, u32[]{:S(2)}, u32[]{:S(2)}) collective-permute-start(bf16[128,1024]{1,0:T(8,128)(2,1)S(1)} %bitcast.29), channel_id=1, source_target_pairs={{0,16},{16,0},{32,48},{48,32},{64,80},{80,64},{96,112},{112,96},{1... | collective-permute-start | bytes 786440 | tf_op jit(solution)/shard_map/ppermute | solution.py:503
  168.9 2.7 %collective-permute-start.9 = (bf16[64,1024]{1,0:T(8,128)(2,1)S(1)}, bf16[64,1024]{1,0:T(8,128)(2,1)S(1)}, u32[]{:S(2)}, u32[]{:S(2)}) collective-permute-start(bf16[64,1024]{1,0:T(8,128)(2,1)S(1)} %slice.42), channel_id=1, source_target_pairs={{0,96},{16,112},{32,0},{48,16},{64,32},{80,48},{96,64},{112,80},{1... | collective-permute-start | bytes 393224 | tf_op jit(solution)/shard_map/ppermute | solution.py:501
  171.6 4.9 %collective-permute-start.11 = (bf16[128,1024]{1,0:T(8,128)(2,1)S(1)}, bf16[128,1024]{1,0:T(8,128)(2,1)S(1)}, u32[]{:S(2)}, u32[]{:S(2)}) collective-permute-start(bf16[128,1024]{1,0:T(8,128)(2,1)S(1)} %collective-permute-done.6.refs_1_), channel_id=1, source_target_pairs={{0,16},{16,0},{32,48},{48,32},{64,80},{80,64},{96,112},{112,96},{1... | collective-permute-start | bytes 786440 | tf_op jit(solution)/shard_map/ppermute | solution.py:503
  176.5 2.8 %collective-permute-start.13 = (bf16[64,1024]{1,0:T(8,128)(2,1)S(1)}, bf16[64,1024]{1,0:T(8,128)(2,1)S(1)}, u32[]{:S(2)}, u32[]{:S(2)}) collective-permute-start(bf16[64,1024]{1,0:T(8,128)(2,1)S(1)} %collective-permute-done.8.refs_3_), channel_id=1, source_target_pairs={{0,16},{16,0},{32,48},{48,32},{64,80},{80,64},{96,112},{112,96},{1... | collective-permute-start | bytes 393224 | tf_op jit(solution)/shard_map/ppermute | solution.py:503
  182.8 2.8 %all-gather.5.cloned.1.call-done.in_ref = bf16[2048,1024]{1,0:T(8,128)(2,1)} async-done(((bf16[128,1024]{1,0:T(8,128)(2,1)}), bf16[2048,1024]{1,0:T(8,128)(2,1)}) %all-gather.5.cloned.1.call-update) | async-done | bytes 4194320 | tf_op jit(solution)/shard_map/all_gather | solution.py:599
  185.6 3.8 %shard_map.115 = bf16[2048,1024]{1,0:T(8,128)(2,1)} custom-call(bf16[2048,1024]{1,0:T(8,128)(2,1)} %all-gather.5.cloned.1.call-done.in_ref), custom_call_target="tpu_custom_call" | custom-call | bytes 8388608 | tf_op jit(solution)/shard_map/pallas_call | solution.py:60
  (78 shorter events, 32.8 us)
Async XLA Ops:
  8.0 34.0 %copy-start.7 = (s32[2048]{0:T(1024)S(1)}, s32[2048]{0:T(1024)}, u32[]{:S(2)}) copy-start(s32[2048]{0:T(1024)} %param.12) | copy-start | bytes 24580
  8.0 87.5 %all-gather.3.cloned.1.call-start = ((), (), s32[]{:S(2)}) async-start(), calls=%async_computation.6 | async-start | bytes 2785280 | tf_op jit(solution)/shard_map/all_gather | solution.py:558
  14.7 32.4 %all-to-all-start = ((bf16[128,4,1024]{2,1,0:T(4,128)(2,1)}), bf16[128,4,1024]{2,1,0:T(4,128)(2,1)S(1)}, u32[]{:S(2)}, u32[]{:S(2)}) async-start(bf16[128,4,1024]{2,1,0:T(4,128)(2,1)} %reshape.49), calls=%async_computation | async-start | bytes 2097152 | tf_op jit(solution)/shard_map/all_to_all | solution.py:35
  26.3 5.4 %collective-permute-start = (f32[16,128]{1,0:T(8,128)S(1)}, f32[16,128]{1,0:T(8,128)S(1)}, u32[]{:S(2)}, u32[]{:S(2)}) collective-permute-start(f32[16,128]{1,0:T(8,128)S(1)} %copy-done.6), channel_id=1, source_target_pairs={{0,1},{1,2},{2,3},{3,0},{4,5},{5,6},{6,7},{7,4},{8,9},{9,10},{10,1... | collective-permute-start | bytes 24584 | tf_op jit(solution)/shard_map/ppermute | solution.py:562
  27.8 6.4 %collective-permute-start.1 = (f32[16,128]{1,0:T(8,128)S(1)}, f32[16,128]{1,0:T(8,128)S(1)}, u32[]{:S(2)}, u32[]{:S(2)}) collective-permute-start(f32[16,128]{1,0:T(8,128)S(1)} %copy-done.6), channel_id=1, source_target_pairs={{0,2},{1,3},{2,0},{3,1},{4,6},{5,7},{6,4},{7,5},{8,10},{9,11},{10,... | collective-permute-start | bytes 24584 | tf_op jit(solution)/shard_map/ppermute | solution.py:562
  30.8 4.2 %collective-permute-start.2 = (f32[16,128]{1,0:T(8,128)S(1)}, f32[16,128]{1,0:T(8,128)S(1)}, u32[]{:S(2)}, u32[]{:S(2)}) collective-permute-start(f32[16,128]{1,0:T(8,128)S(1)} %copy-done.6), channel_id=1, source_target_pairs={{0,3},{1,0},{2,1},{3,2},{4,7},{5,4},{6,5},{7,6},{8,11},{9,8},{10,9... | collective-permute-start | bytes 24584 | tf_op jit(solution)/shard_map/ppermute | solution.py:562
  35.0 7.7 %collective-permute-start.3 = (f32[16,128]{1,0:T(8,128)S(1)}, f32[16,128]{1,0:T(8,128)S(1)}, u32[]{:S(2)}, u32[]{:S(2)}) collective-permute-start(f32[16,128]{1,0:T(8,128)S(1)} %add_add_fusion.1), channel_id=1, source_target_pairs={{0,4},{1,5},{2,6},{3,7},{4,8},{5,9},{6,10},{7,11},{8,12},{9,13},{1... | collective-permute-start | bytes 24584 | tf_op jit(solution)/shard_map/ppermute | solution.py:562
  37.4 5.7 %collective-permute-start.4 = (f32[16,128]{1,0:T(8,128)S(1)}, f32[16,128]{1,0:T(8,128)S(1)}, u32[]{:S(2)}, u32[]{:S(2)}) collective-permute-start(f32[16,128]{1,0:T(8,128)S(1)} %add_add_fusion.1), channel_id=1, source_target_pairs={{0,8},{1,9},{2,10},{3,11},{4,12},{5,13},{6,14},{7,15},{8,0},{9,1},... | collective-permute-start | bytes 24584 | tf_op jit(solution)/shard_map/ppermute | solution.py:562
  40.6 2.9 %collective-permute-start.5 = (f32[16,128]{1,0:T(8,128)S(1)}, f32[16,128]{1,0:T(8,128)S(1)}, u32[]{:S(2)}, u32[]{:S(2)}) collective-permute-start(f32[16,128]{1,0:T(8,128)S(1)} %add_add_fusion.1), channel_id=1, source_target_pairs={{0,12},{1,13},{2,14},{3,15},{4,0},{5,1},{6,2},{7,3},{8,4},{9,5},{1... | collective-permute-start | bytes 24584 | tf_op jit(solution)/shard_map/ppermute | solution.py:562
  58.1 30.6 %all-to-all-start.1 = ((bf16[16,128,384]{2,1,0:T(8,128)(2,1)}), bf16[16,128,384]{2,1,0:T(8,128)(2,1)S(1)}, u32[]{:S(2)}, u32[]{:S(2)}) async-start(bf16[16,128,384]{2,1,0:T(8,128)(2,1)} %bitcast.34), calls=%async_computation.1 | async-start | bytes 3145728 | tf_op jit(solution)/shard_map/all_to_all | solution.py:35
  61.9 67.3 %reduce-scatter.2.cloned.1.call-start = ((), (), s32[]{:S(2)}) async-start(), calls=%async_computation.8 | async-start | bytes 4718592 | tf_op jit(solution)/shard_map/reduce_scatter | solution.py:601
  85.7 28.7 %copy-start.8 = (f32[128]{0:T(128)}, f32[128]{0:T(128)S(1)}, u32[]{:S(2)}) copy-start(f32[128]{0:T(128)S(1)} %fusion.3) | copy-start | bytes 1540
  88.8 36.5 %all-to-all-start.2 = ((bf16[16,128,640]{2,1,0:T(8,128)(2,1)}), bf16[16,128,640]{2,1,0:T(8,128)(2,1)}, u32[]{:S(2)}, u32[]{:S(2)}) async-start(bf16[16,128,640]{2,1,0:T(8,128)(2,1)} %bitcast.32), calls=%async_computation.2 | async-start | bytes 5242880 | tf_op jit(solution)/shard_map/all_to_all | solution.py:35
  93.6 92.0 %all-gather.5.cloned.1.call-start = ((), (), s32[]{:S(2)}) async-start(), calls=%async_computation.7 | async-start | bytes 4456448 | tf_op jit(solution)/shard_map/all_gather | solution.py:599
  131.1 15.1 %all-to-all-start.3 = ((f32[16,8,1152]{2,1,0:T(8,128)}), f32[16,8,1152]{2,1,0:T(8,128)S(1)}, u32[]{:S(2)}, u32[]{:S(2)}) async-start(f32[16,8,1152]{2,1,0:T(8,128)} %pad_maximum_fusion), calls=%async_computation.4 | async-start | bytes 1179648 | tf_op jit(solution)/shard_map/all_to_all | solution.py:35
  157.7 11.0 %collective-permute-start.6 = (bf16[128,1024]{1,0:T(8,128)(2,1)S(1)}, bf16[128,1024]{1,0:T(8,128)(2,1)S(1)}, u32[]{:S(2)}, u32[]{:S(2)}) collective-permute-start(bf16[128,1024]{1,0:T(8,128)(2,1)S(1)} %bitcast.27), channel_id=1, source_target_pairs={{0,32},{16,48},{32,64},{48,80},{64,96},{80,112},{96,0},{112,16},{1... | collective-permute-start | bytes 786440 | tf_op jit(solution)/shard_map/ppermute | solution.py:498
  159.7 9.1 %collective-permute-start.7 = (bf16[128,1024]{1,0:T(8,128)(2,1)S(1)}, bf16[128,1024]{1,0:T(8,128)(2,1)S(1)}, u32[]{:S(2)}, u32[]{:S(2)}) collective-permute-start(bf16[128,1024]{1,0:T(8,128)(2,1)S(1)} %bitcast.28), channel_id=1, source_target_pairs={{0,96},{16,112},{32,0},{48,16},{64,32},{80,48},{96,64},{112,80},{1... | collective-permute-start | bytes 786440 | tf_op jit(solution)/shard_map/ppermute | solution.py:499
  161.2 19.6 %collective-permute-start.10 = (bf16[128,1024]{1,0:T(8,128)(2,1)S(1)}, bf16[128,1024]{1,0:T(8,128)(2,1)S(1)}, u32[]{:S(2)}, u32[]{:S(2)}) collective-permute-start(bf16[128,1024]{1,0:T(8,128)(2,1)S(1)} %bitcast.29), channel_id=1, source_target_pairs={{0,16},{16,0},{32,48},{48,32},{64,80},{80,64},{96,112},{112,96},{1... | collective-permute-start | bytes 786440 | tf_op jit(solution)/shard_map/ppermute | solution.py:503
  168.8 7.7 %collective-permute-start.8 = (bf16[64,1024]{1,0:T(8,128)(2,1)S(1)}, bf16[64,1024]{1,0:T(8,128)(2,1)S(1)}, u32[]{:S(2)}, u32[]{:S(2)}) collective-permute-start(bf16[64,1024]{1,0:T(8,128)(2,1)S(1)} %slice.41), channel_id=1, source_target_pairs={{0,32},{16,48},{32,64},{48,80},{64,96},{80,112},{96,0},{112,16},{1... | collective-permute-start | bytes 393224 | tf_op jit(solution)/shard_map/ppermute | solution.py:500
  168.9 10.5 %collective-permute-start.9 = (bf16[64,1024]{1,0:T(8,128)(2,1)S(1)}, bf16[64,1024]{1,0:T(8,128)(2,1)S(1)}, u32[]{:S(2)}, u32[]{:S(2)}) collective-permute-start(bf16[64,1024]{1,0:T(8,128)(2,1)S(1)} %slice.42), channel_id=1, source_target_pairs={{0,96},{16,112},{32,0},{48,16},{64,32},{80,48},{96,64},{112,80},{1... | collective-permute-start | bytes 393224 | tf_op jit(solution)/shard_map/ppermute | solution.py:501
  171.6 9.2 %collective-permute-start.11 = (bf16[128,1024]{1,0:T(8,128)(2,1)S(1)}, bf16[128,1024]{1,0:T(8,128)(2,1)S(1)}, u32[]{:S(2)}, u32[]{:S(2)}) collective-permute-start(bf16[128,1024]{1,0:T(8,128)(2,1)S(1)} %collective-permute-done.6.refs_1_), channel_id=1, source_target_pairs={{0,16},{16,0},{32,48},{48,32},{64,80},{80,64},{96,112},{112,96},{1... | collective-permute-start | bytes 786440 | tf_op jit(solution)/shard_map/ppermute | solution.py:503
  176.5 4.3 %collective-permute-start.12 = (bf16[128,1024]{1,0:T(8,128)(2,1)S(1)}, bf16[128,1024]{1,0:T(8,128)(2,1)S(1)}, u32[]{:S(2)}, u32[]{:S(2)}) collective-permute-start(bf16[128,1024]{1,0:T(8,128)(2,1)S(1)} %collective-permute-done.7.refs_2_), channel_id=1, source_target_pairs={{0,16},{16,0},{32,48},{48,32},{64,80},{80,64},{96,112},{112,96},{1... | collective-permute-start | bytes 786440 | tf_op jit(solution)/shard_map/ppermute | solution.py:503
  176.5 4.3 %collective-permute-start.13 = (bf16[64,1024]{1,0:T(8,128)(2,1)S(1)}, bf16[64,1024]{1,0:T(8,128)(2,1)S(1)}, u32[]{:S(2)}, u32[]{:S(2)}) collective-permute-start(bf16[64,1024]{1,0:T(8,128)(2,1)S(1)} %collective-permute-done.8.refs_3_), channel_id=1, source_target_pairs={{0,16},{16,0},{32,48},{48,32},{64,80},{80,64},{96,112},{112,96},{1... | collective-permute-start | bytes 393224 | tf_op jit(solution)/shard_map/ppermute | solution.py:503
  179.3 1.4 collective-permute-start.14
  (7 other events, 80.3 us)
Sparse Core Ops, SparseCore 0:
  12.6 66.8 all-gather.2
  129.3 56.2 all-gather.4
Sparse Core Ops, SparseCore 1:
  85.1 39.9 reduce-scatter.1
